TPU v7x, 512 devices: a whole 4x4x16 slice. The times are simulated.
512 devices in a mesh: tab: 8 (over x_hi, y), rad: 64 (over x_lo, z, core).
Axes of the slice: x: 4 (x_hi: 2, x_lo: 2; x = x_hi * 2 + x_lo), y: 4, z: 16, core: 2. Of those that a mesh axis runs over, the one named last changes fastest.
Arguments:
- poloidal: bfloat16 [1024, 16, 2, 2048], P('rad', None, None, 'tab')
- toroidal: bfloat16 [1024, 16, 2, 2048], P('rad', None, None, 'tab')
- tables: bfloat16 [3, 16, 3072, 2048], P(None, None, 'rad', 'tab'), may hold values from -0.125 to 0.125
- orders: int32 [16], replicated, may hold values from 1 to 127, as said below
Outputs:
- velocity: bfloat16 [3, 8, 3072, 6144], P(None, 'tab', 'rad')
Inputs may be any that keep to these rules, and one draw needn't show every extreme that they name: The 16 orders are distinct.
All inputs are finite; a program needn't handle non-finite values.
Results may differ from a plain program's by a relative error of at most 0.02.
Values may be sent and summed in bfloat16 or wider, within the bound.
No kernel may reach another device: no remote copies, remote signals or barrier semaphores. Data moves between devices by JAX's collectives and lax.ppermute only.
A program may use at most 64 MiB of HBM per device.

v0:
```python
import math

import jax
import jax.numpy as jnp
from jax import lax
from jax.sharding import PartitionSpec as P

NPHI = 6144
SHELLS = 8


def radial_rows(levels, shell_count):
    odd_numbers = 2 * jnp.arange(shell_count, dtype=jnp.int32) + 1
    turn_counts = levels[None, :] * odd_numbers[:, None] % (4 * shell_count)
    step_angle = math.pi / (2 * shell_count)
    angles = step_angle * turn_counts.astype(jnp.float32)
    node_angle = step_angle * odd_numbers.astype(jnp.float32)
    value_rows = jnp.cos(angles)
    slope_rows = (
        2.0 * levels.astype(jnp.float32)[None, :] * jnp.sin(angles) / jnp.sin(node_angle)[:, None]
    )
    radius = 1.04 + 0.5 * jnp.cos(node_angle)
    return (value_rows, slope_rows, radius)


def level_terms(value_rows, slope_rows, pol_flat, tor_flat):
    highest = lax.Precision.HIGHEST
    return jnp.stack(
        [
            jnp.dot(value_rows, pol_flat, precision=highest),
            jnp.dot(slope_rows, pol_flat, precision=highest),
            jnp.dot(value_rows, tor_flat, precision=highest),
        ]
    )


def finish(radial, radius, degree_col, order_col):
    degree_wide = degree_col.astype(jnp.float32)
    degree_weight = jnp.where(
        degree_col >= order_col, jnp.sqrt(degree_wide * (degree_wide + 1.0)), 0.0
    )
    spheroidal = radial[0] / radius[:, None]
    radial_term = degree_weight * spheroidal
    horizontal_term = degree_weight * (spheroidal + radial[1])
    toroidal_term = degree_weight * radial[2]
    return jnp.stack([radial_term, horizontal_term, toroidal_term]).astype(jnp.bfloat16)


def combine(plain_part, slope_pol, slope_tor, ratio_pol, ratio_tor):
    theta_part = jnp.stack(
        [slope_pol[:, :, 0] - ratio_tor[:, :, 1], slope_pol[:, :, 1] + ratio_tor[:, :, 0]], axis=2
    )
    phi_part = jnp.stack(
        [-ratio_pol[:, :, 1] - slope_tor[:, :, 0], ratio_pol[:, :, 0] - slope_tor[:, :, 1]], axis=2
    )
    return jnp.stack([plain_part, theta_part, phi_part])


def longitude_table(orders, points):
    positions = jnp.arange(points, dtype=jnp.int32)
    turn_counts = orders[:, None] * positions[None, :] % points
    angles = 2.0 * math.pi / points * turn_counts.astype(jnp.float32)
    return jnp.concatenate([2.0 * jnp.cos(angles), -2.0 * jnp.sin(angles)], axis=0)


def on_device(poloidal, toroidal, tables, orders):
    highest = lax.Precision.HIGHEST
    rad_index = lax.axis_index("rad")
    tab_index = lax.axis_index("tab")
    level_dev = poloidal.shape[0]
    order_count = poloidal.shape[1]
    degree_dev = poloidal.shape[3]
    column_total = order_count * 2 * degree_dev
    column_ids = jnp.arange(column_total, dtype=jnp.int32)
    degree_all = tab_index * degree_dev + column_ids % degree_dev
    order_all = jnp.broadcast_to(orders[:, None, None], (order_count, 2, degree_dev)).reshape(
        column_total
    )
    pol_flat = poloidal.reshape(level_dev, column_total)
    tor_flat = toroidal.reshape(level_dev, column_total)
    levels = rad_index * level_dev + jnp.arange(level_dev, dtype=jnp.int32)
    value_rows, slope_rows, radius = radial_rows(levels, SHELLS)
    partial_value = level_terms(
        value_rows, slope_rows, pol_flat.astype(jnp.float32), tor_flat.astype(jnp.float32)
    )
    radial = lax.psum(partial_value, "rad")
    spectra = finish(radial, radius, degree_all, order_all)
    coefficients = spectra.reshape(3, -1, order_count, 2, degree_dev)

    def project(table_kind, coefficient_kind):
        return jnp.einsum(
            "mal,smcl->sacm",
            tables[table_kind],
            coefficients[coefficient_kind],
            preferred_element_type=jnp.float32,
        )

    fourier = combine(project(0, 0), project(1, 1), project(1, 2), project(2, 1), project(2, 2))
    fourier = fourier.reshape(3, fourier.shape[1], fourier.shape[2], 2 * order_count)
    summed = lax.psum_scatter(
        fourier.astype(jnp.bfloat16), "tab", scatter_dimension=1, tiled=True
    ).astype(jnp.float32)
    phase_table = longitude_table(orders, NPHI)
    values = jnp.dot(summed.reshape(-1, 2 * order_count), phase_table, precision=highest)
    return values.reshape(3, summed.shape[1], summed.shape[2], NPHI).astype(jnp.bfloat16)


def solution(mesh):
    placed = (
        P("rad", None, None, "tab"),
        P("rad", None, None, "tab"),
        P(None, None, "rad", "tab"),
        P(),
    )
    return jax.shard_map(
        on_device,
        mesh=mesh,
        in_specs=placed,
        out_specs=P(None, "tab", "rad", None),
        check_vma=False,
    )
```

profile of v0, /device:TPU:1, one launch (start us, length us, event | category | flops | bytes accessed | tf_op | source)
XLA Modules:
  0.0 529.8 jit_solution(7300522063231394226)
XLA Ops:
  6.5 0.0 all-reduce.4.cloned.1.call-start
  6.6 1.1 reshape.111
  7.7 1.1 reshape.112
  8.9 0.4 convolution_bitcast_fusion.2
  9.3 0.4 convolution_bitcast_fusion
  9.6 0.4 convolution_bitcast_fusion.1
  10.0 0.0 copy-start.1
  10.0 0.9 pad_maximum_fusion
  11.0 0.0 copy-start
  11.0 0.0 all-reduce.4.cloned.1.call-update
  11.0 0.0 all-reduce.6.cloned.1.call-start
  11.0 0.0 copy-done.1
  11.0 0.1 broadcast_bitcast_fusion
  11.2 416.9 %all-reduce.4.cloned.1.call-done = f32[3,8,8192]{2,1,0:T(8,128)} async-done(((f32[3,8,8192]{2,1,0:T(8,128)}), f32[3,8,8192]{2,1,0:T(8,128)}) %all-reduce.4.cloned.1.call-update) | async-done | bytes 786448 | tf_op jit(solution)/shard_map/psum | solution.py:86
  428.2 1.2 multiply_convert_fusion
  429.4 0.0 copy-done
  429.4 0.2 convolution_bitcast_fusion.4
  429.6 0.2 convolution_bitcast_fusion.6
  429.8 0.2 convolution_bitcast_fusion.3
  430.0 0.2 convolution_bitcast_fusion.5
  430.3 0.2 fusion.1
  430.7 0.7 pad_maximum_fusion.1
  431.4 0.0 all-reduce.6.cloned.1.call-update
  431.4 1.7 cosine_multiply_fusion
  433.1 1.3 dynamic-slice
  434.5 84.2 %all-reduce.6.cloned.1.call-done = bf16[3,8,48,32]{2,3,1,0:T(8,128)(2,1)} async-done(((bf16[3,8,48,32]{2,3,1,0:T(8,128)(2,1)}), bf16[3,8,48,32]{2,3,1,0:T(8,128)(2,1)}) %all-reduce.6.cloned.1.call-update) | async-done | bytes 73744
  518.7 4.2 fusion
  (14 shorter events, 0.3 us)
Async XLA Ops:
  6.5 421.6 %all-reduce.4.cloned.1.call-start = ((), (), s32[]{:S(2)}) async-start(), calls=%async_computation | async-start | bytes 1572864 | tf_op jit(solution)/shard_map/psum | solution.py:86
  10.0 1.0 copy-start.1
  11.0 418.4 %copy-start = (bf16[3,16,48,256]{3,2,1,0:T(8,128)(2,1)S(1)}, bf16[3,16,48,256]{3,2,1,0:T(8,128)(2,1)}, u32[]{:S(2)}) copy-start(bf16[3,16,48,256]{3,2,1,0:T(8,128)(2,1)} %param.6) | copy-start | bytes 3538948
  11.0 507.7 %all-reduce.6.cloned.1.call-start = ((), (), s32[]{:S(2)}) async-start(), calls=%async_computation.1 | async-start | bytes 393216
Sparse Core Ops, SparseCore 0:
  11.1 417.0 all-reduce.3
  431.6 87.0 all-reduce.5
where the time goes:
time: 534 us; the launch traced here: 530 us
  waiting for transfers between devices  501 us (94%)
  between operations  13.6 us (3%)
  matrix products  6.4 us (1%)
    psum x1, waiting for transfers between devices, on_device(): radial = lax.psum(partial_value, 'rad')  417 us
    unnamed x3, waiting for transfers between devices  84.3 us
  transfers between devices with their start and end apart: 2, of which 2 were waited for; matrix products, arithmetic and copies ran while one was open for 1% of the time, Pallas kernels for 0%

commit v1 on v0

v1 whole, which is shorter than its diff:
```python
import math

import jax
import jax.numpy as jnp
import numpy as np
from jax import lax
from jax.sharding import Mesh, PartitionSpec as P

NPHI = 6144
SHELLS = 8
RAD = ("xl", "z", "c")
TAB = ("xh", "y")


def radial_rows(levels, shell_count):
    odd_numbers = 2 * jnp.arange(shell_count, dtype=jnp.int32) + 1
    turn_counts = levels[None, :] * odd_numbers[:, None] % (4 * shell_count)
    step_angle = math.pi / (2 * shell_count)
    angles = step_angle * turn_counts.astype(jnp.float32)
    node_angle = step_angle * odd_numbers.astype(jnp.float32)
    value_rows = jnp.cos(angles)
    slope_rows = (
        2.0 * levels.astype(jnp.float32)[None, :] * jnp.sin(angles) / jnp.sin(node_angle)[:, None]
    )
    radius = 1.04 + 0.5 * jnp.cos(node_angle)
    return (value_rows, slope_rows, radius)


def longitude_table(orders, points):
    positions = jnp.arange(points, dtype=jnp.int32)
    turn_counts = orders[:, None] * positions[None, :] % points
    angles = 2.0 * math.pi / points * turn_counts.astype(jnp.float32)
    return jnp.concatenate([2.0 * jnp.cos(angles), -2.0 * jnp.sin(angles)], axis=0)


def split_bf16(x):
    hi = lax.reduce_precision(x, 8, 7)
    return hi.astype(jnp.bfloat16), (x - hi).astype(jnp.bfloat16)


def dot32(a, b):
    return jnp.dot(a, b, preferred_element_type=jnp.float32)


def on_device(poloidal, toroidal, tables, orders):
    xl, z, c = (lax.axis_index(n) for n in RAD)
    tab = lax.axis_index(TAB)
    level_dev, order_count, _, degree_dev = poloidal.shape
    half = order_count // 2
    blocks = half * 2 * degree_dev // 128
    rad_pair = xl * 16 + z
    pol = lax.all_gather(poloidal, "c", axis=0, tiled=True)
    tor = lax.all_gather(toroidal, "c", axis=0, tiled=True)
    pol = lax.dynamic_slice_in_dim(pol, c * half, half, 1).reshape(2 * level_dev, -1)
    tor = lax.dynamic_slice_in_dim(tor, c * half, half, 1).reshape(2 * level_dev, -1)
    levels = rad_pair * 2 * level_dev + jnp.arange(2 * level_dev, dtype=jnp.int32)
    value_rows, slope_rows, radius = radial_rows(levels, SHELLS)
    pol_hi, pol_lo = split_bf16(jnp.concatenate([value_rows, slope_rows]))
    tor_hi, tor_lo = pol_hi[:SHELLS], pol_lo[:SHELLS]
    partial = jnp.concatenate(
        [
            dot32(pol_hi, pol) + dot32(pol_lo, pol),
            dot32(tor_hi, tor) + dot32(tor_lo, tor),
        ]
    ).astype(jnp.bfloat16)
    partial = partial.reshape(3 * SHELLS, blocks, 128).transpose(1, 0, 2)
    shares = lax.all_to_all(partial, ("xl", "z"), 0, 0, tiled=True)
    radial = jnp.sum(shares.astype(jnp.float32), axis=0).reshape(3, SHELLS, 128)

    order = orders[c * half + rad_pair // 4]
    degree = tab * degree_dev + (rad_pair % 2) * 128 + jnp.arange(128, dtype=jnp.int32)
    degree_wide = degree.astype(jnp.float32)
    weight = jnp.where(degree >= order, jnp.sqrt(degree_wide * (degree_wide + 1.0)), 0.0)
    spheroidal = radial[0] / radius[:, None]
    spectra = jnp.stack(
        [weight * spheroidal, weight * (spheroidal + radial[1]), weight * radial[2]]
    ).astype(jnp.bfloat16)
    spectra = jnp.broadcast_to(spectra.reshape(1, 3 * SHELLS, 128), (blocks, 3 * SHELLS, 128))
    spectra = lax.all_to_all(spectra, ("xl", "z"), 0, 0, tiled=True)
    spectra = lax.all_gather(spectra, "c", axis=0, tiled=True)
    coef = spectra.reshape(order_count, 2, 2, 3, SHELLS, 128).transpose(3, 0, 4, 1, 2, 5)
    coef = coef.reshape(3, order_count, SHELLS, 2, degree_dev)

    q, s, t = coef[0], coef[1], coef[2]
    swap = lambda v: jnp.stack([-v[:, :, 1], v[:, :, 0]], axis=2)
    theta = jnp.concatenate([s, swap(t)], axis=-1)
    phi = jnp.concatenate([-t, swap(s)], axis=-1)
    both = jnp.concatenate([theta, phi], axis=1)
    pair_table = jnp.concatenate([tables[1], tables[2]], axis=-1)
    plain = jnp.einsum("mscl,mal->mcsa", q, tables[0], preferred_element_type=jnp.float32)
    pair = jnp.einsum("mscl,mal->mcsa", both, pair_table, preferred_element_type=jnp.float32)
    fourier = jnp.stack([plain, pair[:, :, :SHELLS], pair[:, :, SHELLS:]])
    fourier = fourier.transpose(3, 2, 1, 0, 4).reshape(SHELLS, 2 * order_count, -1)
    fourier = lax.all_to_all(fourier.astype(jnp.bfloat16), TAB, 0, 0, tiled=True)
    summed = jnp.sum(fourier.astype(jnp.float32), axis=0)
    f_hi, f_lo = split_bf16(summed)
    p_hi, p_lo = split_bf16(longitude_table(orders, NPHI))
    values = lax.dot_general(
        jnp.concatenate([f_hi, f_hi, f_lo]),
        jnp.concatenate([p_hi, p_lo, p_hi]),
        (((0,), (0,)), ((), ())),
        preferred_element_type=jnp.float32,
    )
    return values.astype(jnp.bfloat16).reshape(3, 1, -1, NPHI)


def solution(mesh):
    fine = Mesh(mesh.devices.reshape(2, 4, 2, 16, 2), TAB + RAD)
    placed = (
        P(RAD, None, None, TAB),
        P(RAD, None, None, TAB),
        P(None, None, RAD, TAB),
        P(),
    )
    return jax.shard_map(
        on_device,
        mesh=fine,
        in_specs=placed,
        out_specs=P(None, TAB, RAD, None),
        check_vma=False,
    )
```

time: 534 us -> 88.7 us (0.17)
  waiting for transfers between devices: 501 us -> 38 us
  starting transfers between devices: 0.04 us -> 21.5 us
  blocking collectives: 0 us -> 16.7 us
  between operations: 13.6 us -> 0.27 us
    psum x1 -> x0, waiting for transfers between devices: 417 us -> none  [on_device(): radial = lax.psum(partial_value, 'rad')]
    unnamed x3 -> x0, waiting for transfers between devices: 84.3 us -> none
    all_to_all x0 -> x3, waiting for transfers between devices: none -> 38 us  [the longest x1 16.5 us: on_device(): shares = lax.all_to_all(partial, ('xl', 'z'), 0, 0, tiled=True)]
    all_to_all x0 -> x3, starting transfers between devices: none -> 21.5 us  [the longest x1 10.8 us: on_device(): shares = lax.all_to_all(partial, ('xl', 'z'), 0, 0, tiled=True)]
    all_gather x0 -> x3, blocking collectives: none -> 16.7 us  [the longest x1 8.69 us: on_device(): pol = lax.all_gather(poloidal, 'c', axis=0, tiled=True)]
  transfers between devices with their start and end apart: 2 -> 3, of which waited for: 2 -> 3; matrix products, arithmetic and copies ran while one was open for 1% -> 4% of each run, Pallas kernels for 0% -> 0%
where the time goes in v1:
time: 88.7 us; the launch traced here: 88.3 us
  waiting for transfers between devices  38 us (43%)
  starting transfers between devices  21.5 us (24%)
  blocking collectives  16.7 us (19%)
  local copies, waits for them, and re-layouts  5.24 us (6%)
  other arithmetic  3.6 us (4%)
  matrix products  3 us (3%)
    all_to_all x1, waiting for transfers between devices, on_device(): shares = lax.all_to_all(partial, ('xl', 'z'), 0, 0, tiled=True)  16.5 us
    all_to_all x1, waiting for transfers between devices, on_device(): spectra = lax.all_to_all(spectra, ('xl', 'z'), 0, 0, tiled=True)  14.6 us
    all_to_all x1, starting transfers between devices, on_device(): shares = lax.all_to_all(partial, ('xl', 'z'), 0, 0, tiled=True)  10.8 us
    all_gather x1, blocking collectives, on_device(): pol = lax.all_gather(poloidal, 'c', axis=0, tiled=True)  8.69 us
    all_to_all x1, waiting for transfers between devices, on_device(): lax.all_to_all(fourier.astype(jnp.bfloat16), TAB, 0, 0, tiled=True)  6.84 us
    all_to_all x1, starting transfers between devices, on_device(): lax.all_to_all(fourier.astype(jnp.bfloat16), TAB, 0, 0, tiled=True)  6.35 us
    all_gather x1, blocking collectives, on_device(): spectra = lax.all_gather(spectra, 'c', axis=0, tiled=True)  5.82 us
    all_to_all x1, starting transfers between devices, on_device(): spectra = lax.all_to_all(spectra, ('xl', 'z'), 0, 0, tiled=True)  4.35 us
  transfers between devices with their start and end apart: 3, of which 3 were waited for; matrix products, arithmetic and copies ran while one was open for 4% of the time, Pallas kernels for 0%

profile of v1, /device:TPU:1, one launch (start us, length us, event | category | flops | bytes accessed | tf_op | source)
XLA Modules:
  0.0 88.3 jit_solution(1885416919202241246)
XLA Ops:
  0.1 1.0 %copy.15 = bf16[16,16,2,256]{3,1,2,0:T(8,128)(2,1)S(1)} copy(bf16[16,16,2,256]{3,2,1,0:T(2,128)(2,1)} %param.4) | data formatting | bytes 524288 | tf_op args[0]
  1.1 8.7 %all_gather.9 = bf16[32,16,2,256]{3,1,2,0:T(8,128)(2,1)S(1)} all-gather(bf16[16,16,2,256]{3,1,2,0:T(8,128)(2,1)S(1)} %copy.15), channel_id=1, replica_groups=mesh['xh'=2,'y'=4,'xl'=2,'z'=16,'c'=2] {'c'}, dimensions={0}, use_global_device_ids=true | all-gather | bytes 786432 | tf_op jit(solution)/shard_map/all_gather | solution.py:52
  9.7 1.0 %copy.17 = bf16[16,16,2,256]{3,1,2,0:T(8,128)(2,1)S(1)} copy(bf16[16,16,2,256]{3,2,1,0:T(2,128)(2,1)} %param.5) | data formatting | bytes 524288 | tf_op args[1]
  10.7 2.2 %all_gather.10 = bf16[32,16,2,256]{3,1,2,0:T(8,128)(2,1)S(1)} all-gather(bf16[16,16,2,256]{3,1,2,0:T(8,128)(2,1)S(1)} %copy.17), channel_id=1, replica_groups=mesh['xh'=2,'y'=4,'xl'=2,'z'=16,'c'=2] {'c'}, dimensions={0}, use_global_device_ids=true | all-gather | bytes 786432 | tf_op jit(solution)/shard_map/all_gather | solution.py:53
  13.0 0.2 copy.18
  13.2 0.2 reshape.120
  13.3 0.2 copy.16
  13.6 0.2 reshape.119
  13.7 0.1 fusion.51
  13.9 0.0 copy-start.1
  13.9 0.2 fusion.49
  14.0 0.2 fusion.57
  14.2 0.2 fusion.9
  14.4 0.0 copy-start
  14.4 0.2 fusion.7
  14.6 0.7 maximum_bitcast_fusion.2
  15.3 10.8 %all-to-all-start = ((bf16[32,24,128]{2,1,0:T(8,128)(2,1)}), bf16[32,24,128]{2,1,0:T(8,128)(2,1)S(1)}, u32[]{:S(2)}, u32[]{:S(2)}) async-start(bf16[32,24,128]{2,1,0:T(8,128)(2,1)} %maximum_bitcast_fusion.2), calls=%async_computation | async-start | bytes 393216 | tf_op jit(solution)/shard_map/all_to_all | solution.py:67
  26.1 0.0 copy-done.1
  26.1 0.6 dynamic_slice.9
  26.8 0.6 compare_select_fusion
  27.4 16.5 %all-to-all-done = bf16[32,24,128]{2,1,0:T(8,128)(2,1)S(1)} async-done(((bf16[32,24,128]{2,1,0:T(8,128)(2,1)}), bf16[32,24,128]{2,1,0:T(8,128)(2,1)S(1)}, u32[]{:S(2)}, u32[]{:S(2)}) %all-to-all-start) | async-done | bytes 196640 | tf_op jit(solution)/shard_map/all_to_all | solution.py:67
  44.0 0.1 fusion.45
  44.1 0.7 broadcast_in_dim.7
  44.8 4.4 %all-to-all-start.1 = ((bf16[32,24,128]{2,1,0:T(8,128)(2,1)}), bf16[32,24,128]{2,1,0:T(8,128)(2,1)S(1)}, u32[]{:S(2)}, u32[]{:S(2)}) async-start(bf16[32,24,128]{2,1,0:T(8,128)(2,1)} %broadcast_in_dim.7), calls=%async_computation.1 | async-start | bytes 393216 | tf_op jit(solution)/shard_map/all_to_all | solution.py:79
  49.1 1.7 %cosine_multiply_fusion = (f32[16,6144]{1,0:T(8,128)S(1)}, f32[16,6144]{1,0:T(8,128)S(1)}) fusion(s32[16]{0:T(128)S(1)} %copy-done.1), kind=kLoop, calls=%fused_computation.39 | loop fusion | flops 1081344 | bytes 786496 | tf_op jit(solution)/shard_map/mul | solution.py:33
  50.8 0.0 copy-done
  50.8 0.1 slice_bitcast_fusion.1
  50.9 14.6 %all-to-all-done.1 = bf16[32,24,128]{2,1,0:T(8,128)(2,1)S(1)} async-done(((bf16[32,24,128]{2,1,0:T(8,128)(2,1)}), bf16[32,24,128]{2,1,0:T(8,128)(2,1)S(1)}, u32[]{:S(2)}, u32[]{:S(2)}) %all-to-all-start.1) | async-done | bytes 196640 | tf_op jit(solution)/shard_map/all_to_all | solution.py:79
  65.5 5.8 %all_gather.11 = bf16[64,24,128]{2,1,0:T(8,128)(2,1)S(1)} all-gather(bf16[32,24,128]{2,1,0:T(8,128)(2,1)S(1)} %all-to-all-done.1), channel_id=1, replica_groups=mesh['xh'=2,'y'=4,'xl'=2,'z'=16,'c'=2] {'c'}, dimensions={0}, use_global_device_ids=true | all-gather | bytes 589824 | tf_op jit(solution)/shard_map/all_gather | solution.py:80
  71.4 0.2 fusion.10
  71.7 0.3 fusion.8
  72.1 0.2 copy.20
  72.3 0.8 convert_element_type.85
  73.1 6.4 %all-to-all-start.2 = ((bf16[8,32,144]{2,1,0:T(8,128)(2,1)}), bf16[8,32,144]{2,1,0:T(8,128)(2,1)S(1)}, u32[]{:S(2)}, u32[]{:S(2)}) async-start(bf16[8,32,144]{2,1,0:T(8,128)(2,1)} %convert_element_type.85), calls=%async_computation.2 | async-start | bytes 262144 | tf_op jit(solution)/shard_map/all_to_all | solution.py:94
  79.4 0.1 fusion.11
  79.5 6.8 %all-to-all-done.2 = bf16[8,32,144]{2,1,0:T(8,128)(2,1)S(1)} async-done(((bf16[8,32,144]{2,1,0:T(8,128)(2,1)}), bf16[8,32,144]{2,1,0:T(8,128)(2,1)S(1)}, u32[]{:S(2)}, u32[]{:S(2)}) %all-to-all-start.2) | async-done | bytes 73760 | tf_op jit(solution)/shard_map/all_to_all | solution.py:94
  86.4 1.9 %convolution_convert_fusion = bf16[144,6144]{1,0:T(8,128)(2,1)} fusion(bf16[32,6144]{1,0:T(8,128)(2,1)S(1)} %get-tuple-element.8, bf16[32,6144]{1,0:T(8,128)(2,1)S(1)} %get-tuple-element.7, bf16[32,144]{1,0:T(8,128)(2,1)S(1)} %get-tuple-element.18, bf16[32,144]{1,0:T(8,128)(2,1)S(1)} %get-tuple-element.17), kind=kOutput, calls=%fused_computation | convolution fusion | flops 174375936 | bytes 2574336 | tf_op jit(solution)/shard_map/dot_general | solution.py:98
  (18 shorter events, 0.4 us)
Async XLA Ops:
  13.9 12.2 %copy-start.1 = (s32[16]{0:T(128)S(1)}, s32[16]{0:T(128)}, u32[]{:S(2)}) copy-start(s32[16]{0:T(128)} %param.7) | copy-start | bytes 196
  14.4 36.4 %copy-start = (bf16[3,16,48,256]{3,2,1,0:T(8,128)(2,1)S(1)}, bf16[3,16,48,256]{3,2,1,0:T(8,128)(2,1)}, u32[]{:S(2)}) copy-start(bf16[3,16,48,256]{3,2,1,0:T(8,128)(2,1)} %param.6) | copy-start | bytes 3538948
  15.3 28.6 %all-to-all-start = ((bf16[32,24,128]{2,1,0:T(8,128)(2,1)}), bf16[32,24,128]{2,1,0:T(8,128)(2,1)S(1)}, u32[]{:S(2)}, u32[]{:S(2)}) async-start(bf16[32,24,128]{2,1,0:T(8,128)(2,1)} %maximum_bitcast_fusion.2), calls=%async_computation | async-start | bytes 393216 | tf_op jit(solution)/shard_map/all_to_all | solution.py:67
  44.8 20.8 %all-to-all-start.1 = ((bf16[32,24,128]{2,1,0:T(8,128)(2,1)}), bf16[32,24,128]{2,1,0:T(8,128)(2,1)S(1)}, u32[]{:S(2)}, u32[]{:S(2)}) async-start(bf16[32,24,128]{2,1,0:T(8,128)(2,1)} %broadcast_in_dim.7), calls=%async_computation.1 | async-start | bytes 393216 | tf_op jit(solution)/shard_map/all_to_all | solution.py:79
  73.1 13.3 %all-to-all-start.2 = ((bf16[8,32,144]{2,1,0:T(8,128)(2,1)}), bf16[8,32,144]{2,1,0:T(8,128)(2,1)S(1)}, u32[]{:S(2)}, u32[]{:S(2)}) async-start(bf16[8,32,144]{2,1,0:T(8,128)(2,1)} %convert_element_type.85), calls=%async_computation.2 | async-start | bytes 262144 | tf_op jit(solution)/shard_map/all_to_all | solution.py:94

commit v2 on v1

--- a/solution.py
+++ b/solution.py
@@ -2,8 +2,9 @@
 
 import jax
 import jax.numpy as jnp
-import numpy as np
 from jax import lax
+from jax.experimental import pallas as pl
+from jax.experimental.pallas import tpu as pltpu
 from jax.sharding import Mesh, PartitionSpec as P
 
 NPHI = 6144
@@ -12,18 +13,53 @@
 TAB = ("xh", "y")
 
 
-def radial_rows(levels, shell_count):
-    odd_numbers = 2 * jnp.arange(shell_count, dtype=jnp.int32) + 1
-    turn_counts = levels[None, :] * odd_numbers[:, None] % (4 * shell_count)
-    step_angle = math.pi / (2 * shell_count)
-    angles = step_angle * turn_counts.astype(jnp.float32)
-    node_angle = step_angle * odd_numbers.astype(jnp.float32)
-    value_rows = jnp.cos(angles)
-    slope_rows = (
-        2.0 * levels.astype(jnp.float32)[None, :] * jnp.sin(angles) / jnp.sin(node_angle)[:, None]
-    )
-    radius = 1.04 + 0.5 * jnp.cos(node_angle)
-    return (value_rows, slope_rows, radius)
+def shell_radius():
+    return 1.04 + 0.5 * jnp.cos(math.pi / (2 * SHELLS) * (2 * jnp.arange(SHELLS) + 1))
+
+
+def level_matrix(first_level, level_dev):
+    shape = (2 * 3 * SHELLS, 4 * level_dev * 2)
+    row = lax.broadcasted_iota(jnp.int32, shape, 0)
+    col = lax.broadcasted_iota(jnp.int32, shape, 1)
+    kind = row % (3 * SHELLS) // SHELLS
+    odd = 2 * (row % SHELLS) + 1
+    level = first_level + col % (2 * level_dev) // 2
+    source = col // (2 * level_dev)
+    step_angle = math.pi / (2 * SHELLS)
+    angle = step_angle * (level * odd % (4 * SHELLS)).astype(jnp.float32)
+    node_angle = step_angle * odd.astype(jnp.float32)
+    slope = 2.0 * level.astype(jnp.float32) * jnp.sin(angle) / jnp.sin(node_angle)
+    entry = jnp.where(kind == 1, slope, jnp.cos(angle))
+    high = lax.reduce_precision(entry, 8, 7)
+    entry = jnp.where(source % 2 == 0, high, entry - high)
+    used = (row // (3 * SHELLS) == col % 2) & ((kind < 2) == (source < 2))
+    return jnp.where(used, entry, 0.0).astype(jnp.bfloat16)
+
+
+def level_kernel(matrix_ref, pol_ref, tor_ref, out_ref):
+    level_dev, order_count, _, degree_dev = pol_ref.shape
+    rows = out_ref.shape[1]
+    matrix = matrix_ref[...]
+    for order in range(order_count):
+        pol = pol_ref[:, order].reshape(2 * level_dev, degree_dev)
+        tor = tor_ref[:, order].reshape(2 * level_dev, degree_dev)
+        sums = dot32(matrix, jnp.concatenate([pol, pol, tor, tor], axis=0))
+        for part in range(2):
+            for cut in range(degree_dev // 128):
+                block = sums[part * rows : (part + 1) * rows, cut * 128 : (cut + 1) * 128]
+                out_ref[(order * 2 + part) * (degree_dev // 128) + cut] = block.astype(jnp.bfloat16)
+
+
+def level_sums(matrix, poloidal, toroidal):
+    _, order_count, _, degree_dev = poloidal.shape
+    return pl.pallas_call(
+        level_kernel,
+        out_shape=jax.ShapeDtypeStruct(
+            (order_count * 2 * degree_dev // 128, 3 * SHELLS, 128), jnp.bfloat16
+        ),
+        compiler_params=pltpu.CompilerParams(vmem_limit_bytes=60 << 20),
+        name="level_sums",
+    )(matrix, poloidal, toroidal)
 
 
 def longitude_table(orders, points):
@@ -49,21 +85,11 @@
     half = order_count // 2
     blocks = half * 2 * degree_dev // 128
     rad_pair = xl * 16 + z
-    pol = lax.all_gather(poloidal, "c", axis=0, tiled=True)
-    tor = lax.all_gather(toroidal, "c", axis=0, tiled=True)
-    pol = lax.dynamic_slice_in_dim(pol, c * half, half, 1).reshape(2 * level_dev, -1)
-    tor = lax.dynamic_slice_in_dim(tor, c * half, half, 1).reshape(2 * level_dev, -1)
-    levels = rad_pair * 2 * level_dev + jnp.arange(2 * level_dev, dtype=jnp.int32)
-    value_rows, slope_rows, radius = radial_rows(levels, SHELLS)
-    pol_hi, pol_lo = split_bf16(jnp.concatenate([value_rows, slope_rows]))
-    tor_hi, tor_lo = pol_hi[:SHELLS], pol_lo[:SHELLS]
-    partial = jnp.concatenate(
-        [
-            dot32(pol_hi, pol) + dot32(pol_lo, pol),
-            dot32(tor_hi, tor) + dot32(tor_lo, tor),
-        ]
-    ).astype(jnp.bfloat16)
-    partial = partial.reshape(3 * SHELLS, blocks, 128).transpose(1, 0, 2)
+    matrix = level_matrix((rad_pair * 2 + c) * level_dev, level_dev)
+    partial = level_sums(matrix, poloidal, toroidal)
+    pair = lax.all_gather(partial, "c", axis=0)
+    pair = lax.dynamic_slice_in_dim(pair, c * blocks, blocks, 1).astype(jnp.float32)
+    partial = (pair[0] + pair[1]).astype(jnp.bfloat16)
     shares = lax.all_to_all(partial, ("xl", "z"), 0, 0, tiled=True)
     radial = jnp.sum(shares.astype(jnp.float32), axis=0).reshape(3, SHELLS, 128)
 
@@ -71,7 +97,7 @@
     degree = tab * degree_dev + (rad_pair % 2) * 128 + jnp.arange(128, dtype=jnp.int32)
     degree_wide = degree.astype(jnp.float32)
     weight = jnp.where(degree >= order, jnp.sqrt(degree_wide * (degree_wide + 1.0)), 0.0)
-    spheroidal = radial[0] / radius[:, None]
+    spheroidal = radial[0] / shell_radius()[:, None]
     spectra = jnp.stack(
         [weight * spheroidal, weight * (spheroidal + radial[1]), weight * radial[2]]
     ).astype(jnp.bfloat16)

time: 88.7 us -> 86.4 us (0.974)
  local copies, waits for them, and re-layouts: 5.24 us -> 2.49 us
  Pallas kernels: 0 us -> 2.12 us
  blocking collectives: 16.7 us -> 14.9 us
  other arithmetic: 3.6 us -> 4.54 us
    pallas_call x0 -> x1, Pallas kernels: none -> 2.12 us  [level_sums(): pl.pallas_call(level_kernel, out_shape=jax.ShapeDtypeStruct((order_count...]
    unnamed x6 -> x4, local copies, waits for them, and re-layouts: 1.97 us -> 0.01 us
    all_gather x2 -> x1, blocking collectives: 10.9 us -> 9.06 us  [on_device(): pair = lax.all_gather(partial, 'c', axis=0)]
    convert_element_type x0 -> x3, other arithmetic: none -> 1.69 us  [the longest x1 0.92 us: level_matrix(): return jnp.where(used, entry, 0.0).astype(jnp.bfloat16)]
where the time goes in v2:
time: 86.4 us; the launch traced here: 86 us
  waiting for transfers between devices  37.9 us (44%)
  starting transfers between devices  21.5 us (25%)
  blocking collectives  14.9 us (17%)
  other arithmetic  4.54 us (5%)
  local copies, waits for them, and re-layouts  2.49 us (3%)
  matrix products  2.37 us (3%)
  Pallas kernels  2.12 us (2%)
    all_to_all x1, waiting for transfers between devices, on_device(): shares = lax.all_to_all(partial, ('xl', 'z'), 0, 0, tiled=True)  16.4 us
    all_to_all x1, waiting for transfers between devices, on_device(): spectra = lax.all_to_all(spectra, ('xl', 'z'), 0, 0, tiled=True)  14.6 us
    all_to_all x1, starting transfers between devices, on_device(): shares = lax.all_to_all(partial, ('xl', 'z'), 0, 0, tiled=True)  10.8 us
    all_gather x1, blocking collectives, on_device(): pair = lax.all_gather(partial, 'c', axis=0)  9.06 us
    all_to_all x1, waiting for transfers between devices, on_device(): lax.all_to_all(fourier.astype(jnp.bfloat16), TAB, 0, 0, tiled=True)  6.84 us
    all_to_all x1, starting transfers between devices, on_device(): lax.all_to_all(fourier.astype(jnp.bfloat16), TAB, 0, 0, tiled=True)  6.35 us
    all_gather x1, blocking collectives, on_device(): spectra = lax.all_gather(spectra, 'c', axis=0, tiled=True)  5.82 us
    all_to_all x1, starting transfers between devices, on_device(): spectra = lax.all_to_all(spectra, ('xl', 'z'), 0, 0, tiled=True)  4.36 us
  transfers between devices with their start and end apart: 3, of which 3 were waited for; matrix products, arithmetic and copies ran while one was open for 4% of the time, Pallas kernels for 0%

profile of v2, /device:TPU:1, one launch (start us, length us, event | category | flops | bytes accessed | tf_op | source)
XLA Modules:
  0.0 86.0 jit_solution(6920264940603845811)
XLA Ops:
  0.1 0.9 %fusion.44.matrix_ref = bf16[48,128]{1,0:T(8,128)(2,1)} fusion(s32[48]{0:T(128)S(1)} %get-tuple-element.34, s32[48]{0:T(128)S(1)} %get-tuple-element.35, s32[128]{0:T(128)S(1)} %get-tuple-element.29, s32[128]{0:T(128)S(1)} %get-tuple-element.31, s32[]{:T(128)S(6)} %mul.146, s32[128]{0:T(128)S(1)} %get-tuple-element.28, s32[128]{0:T(128)S(1)} %get-tuple-element.36, ...), kind=kLoop, calls=%fused_computation.95 | loop fusion | flops 509952 | bytes 17044 | tf_op jit(solution)/shard_map/convert_element_type | solution.py:36
  1.1 2.1 %level_sums.1 = bf16[64,24,128]{2,1,0:T(8,128)(2,1)} custom-call(bf16[48,128]{1,0:T(8,128)(2,1)} %fusion.44.matrix_ref, bf16[16,16,2,256]{3,2,1,0:T(2,128)(2,1)} %pol_ref.1, bf16[16,16,2,256]{3,2,1,0:T(2,128)(2,1)} %tor_ref.1), custom_call_target="tpu_custom_call" | custom-call | tf_op jit(solution)/shard_map/level_sums/pallas_call | solution.py:55
  3.2 9.1 %all-gather = bf16[128,24,128]{2,1,0:T(8,128)(2,1)S(1)} all-gather(bf16[64,24,128]{2,1,0:T(8,128)(2,1)} %level_sums.1), channel_id=2, replica_groups=mesh['xh'=2,'y'=4,'xl'=2,'z'=16,'c'=2] {'c'}, dimensions={0}, use_global_device_ids=true | all-gather | bytes 1179648 | tf_op jit(solution)/shard_map/all_gather | solution.py:90
  12.2 0.0 copy-start.1
  12.2 0.1 dynamic-slice_convert_fusion
  12.3 0.0 copy-start
  12.3 0.7 fusion.29
  13.0 10.8 %all-to-all-start = ((bf16[32,24,128]{2,1,0:T(8,128)(2,1)}), bf16[32,24,128]{2,1,0:T(8,128)(2,1)S(1)}, u32[]{:S(2)}, u32[]{:S(2)}) async-start(bf16[32,24,128]{2,1,0:T(8,128)(2,1)} %fusion.29), calls=%async_computation | async-start | bytes 393216 | tf_op jit(solution)/shard_map/all_to_all | solution.py:93
  23.8 0.0 copy-done.1
  23.8 0.7 dynamic_slice.6
  24.6 0.7 compare_select_fusion
  25.3 16.4 %all-to-all-done = bf16[32,24,128]{2,1,0:T(8,128)(2,1)S(1)} async-done(((bf16[32,24,128]{2,1,0:T(8,128)(2,1)}), bf16[32,24,128]{2,1,0:T(8,128)(2,1)S(1)}, u32[]{:S(2)}, u32[]{:S(2)}) %all-to-all-start) | async-done | bytes 196640 | tf_op jit(solution)/shard_map/all_to_all | solution.py:93
  41.7 0.1 fusion.59
  41.8 0.7 broadcast_in_dim.12
  42.5 4.4 %all-to-all-start.1 = ((bf16[32,24,128]{2,1,0:T(8,128)(2,1)}), bf16[32,24,128]{2,1,0:T(8,128)(2,1)S(1)}, u32[]{:S(2)}, u32[]{:S(2)}) async-start(bf16[32,24,128]{2,1,0:T(8,128)(2,1)} %broadcast_in_dim.12), calls=%async_computation.1 | async-start | bytes 393216 | tf_op jit(solution)/shard_map/all_to_all | solution.py:105
  46.9 1.7 %cosine_multiply_fusion = (f32[16,6144]{1,0:T(8,128)S(1)}, f32[16,6144]{1,0:T(8,128)S(1)}) fusion(s32[16]{0:T(128)S(1)} %copy-done.1), kind=kLoop, calls=%fused_computation.35 | loop fusion | flops 1081344 | bytes 786496 | tf_op jit(solution)/shard_map/mul | solution.py:69
  48.6 0.0 copy-done
  48.6 0.1 slice_bitcast_fusion.1
  48.6 14.6 %all-to-all-done.1 = bf16[32,24,128]{2,1,0:T(8,128)(2,1)S(1)} async-done(((bf16[32,24,128]{2,1,0:T(8,128)(2,1)}), bf16[32,24,128]{2,1,0:T(8,128)(2,1)S(1)}, u32[]{:S(2)}, u32[]{:S(2)}) %all-to-all-start.1) | async-done | bytes 196640 | tf_op jit(solution)/shard_map/all_to_all | solution.py:105
  63.3 5.8 %all_gather.11 = bf16[64,24,128]{2,1,0:T(8,128)(2,1)S(1)} all-gather(bf16[32,24,128]{2,1,0:T(8,128)(2,1)S(1)} %all-to-all-done.1), channel_id=1, replica_groups=mesh['xh'=2,'y'=4,'xl'=2,'z'=16,'c'=2] {'c'}, dimensions={0}, use_global_device_ids=true | all-gather | bytes 589824 | tf_op jit(solution)/shard_map/all_gather | solution.py:106
  69.1 0.2 fusion.6
  69.4 0.3 fusion.5
  69.8 0.2 copy.8
  70.0 0.8 convert_element_type.86
  70.8 6.4 %all-to-all-start.2 = ((bf16[8,32,144]{2,1,0:T(8,128)(2,1)}), bf16[8,32,144]{2,1,0:T(8,128)(2,1)S(1)}, u32[]{:S(2)}, u32[]{:S(2)}) async-start(bf16[8,32,144]{2,1,0:T(8,128)(2,1)} %convert_element_type.86), calls=%async_computation.2 | async-start | bytes 262144 | tf_op jit(solution)/shard_map/all_to_all | solution.py:120
  77.2 0.1 fusion.7
  77.3 6.8 %all-to-all-done.2 = bf16[8,32,144]{2,1,0:T(8,128)(2,1)S(1)} async-done(((bf16[8,32,144]{2,1,0:T(8,128)(2,1)}), bf16[8,32,144]{2,1,0:T(8,128)(2,1)S(1)}, u32[]{:S(2)}, u32[]{:S(2)}) %all-to-all-start.2) | async-done | bytes 73760 | tf_op jit(solution)/shard_map/all_to_all | solution.py:120
  84.2 1.9 %convolution_convert_fusion = bf16[144,6144]{1,0:T(8,128)(2,1)} fusion(bf16[32,6144]{1,0:T(8,128)(2,1)S(1)} %get-tuple-element.8, bf16[32,6144]{1,0:T(8,128)(2,1)S(1)} %get-tuple-element.7, bf16[32,144]{1,0:T(8,128)(2,1)S(1)} %get-tuple-element.18, bf16[32,144]{1,0:T(8,128)(2,1)S(1)} %get-tuple-element.17), kind=kOutput, calls=%fused_computation | convolution fusion | flops 174375936 | bytes 2574336 | tf_op jit(solution)/shard_map/dot_general | solution.py:124
  (21 shorter events, 0.3 us)
Async XLA Ops:
  12.2 11.6 %copy-start.1 = (s32[16]{0:T(128)S(1)}, s32[16]{0:T(128)}, u32[]{:S(2)}) copy-start(s32[16]{0:T(128)} %param.7) | copy-start | bytes 196
  12.3 36.3 %copy-start = (bf16[3,16,48,256]{3,2,1,0:T(8,128)(2,1)S(1)}, bf16[3,16,48,256]{3,2,1,0:T(8,128)(2,1)}, u32[]{:S(2)}) copy-start(bf16[3,16,48,256]{3,2,1,0:T(8,128)(2,1)} %param.6) | copy-start | bytes 3538948
  13.0 28.6 %all-to-all-start = ((bf16[32,24,128]{2,1,0:T(8,128)(2,1)}), bf16[32,24,128]{2,1,0:T(8,128)(2,1)S(1)}, u32[]{:S(2)}, u32[]{:S(2)}) async-start(bf16[32,24,128]{2,1,0:T(8,128)(2,1)} %fusion.29), calls=%async_computation | async-start | bytes 393216 | tf_op jit(solution)/shard_map/all_to_all | solution.py:93
  42.5 20.8 %all-to-all-start.1 = ((bf16[32,24,128]{2,1,0:T(8,128)(2,1)}), bf16[32,24,128]{2,1,0:T(8,128)(2,1)S(1)}, u32[]{:S(2)}, u32[]{:S(2)}) async-start(bf16[32,24,128]{2,1,0:T(8,128)(2,1)} %broadcast_in_dim.12), calls=%async_computation.1 | async-start | bytes 393216 | tf_op jit(solution)/shard_map/all_to_all | solution.py:105
  70.8 13.3 %all-to-all-start.2 = ((bf16[8,32,144]{2,1,0:T(8,128)(2,1)}), bf16[8,32,144]{2,1,0:T(8,128)(2,1)S(1)}, u32[]{:S(2)}, u32[]{:S(2)}) async-start(bf16[8,32,144]{2,1,0:T(8,128)(2,1)} %convert_element_type.86), calls=%async_computation.2 | async-start | bytes 262144 | tf_op jit(solution)/shard_map/all_to_all | solution.py:120

commit v3 on v2

--- a/solution.py
+++ b/solution.py
@@ -9,7 +9,8 @@
 
 NPHI = 6144
 SHELLS = 8
-RAD = ("xl", "z", "c")
+RAD = ("xl", "zf", "zn", "c")
+NEAR = ("xl", "zn")
 TAB = ("xh", "y")
 
 
@@ -79,30 +80,46 @@
 
 
 def on_device(poloidal, toroidal, tables, orders):
-    xl, z, c = (lax.axis_index(n) for n in RAD)
+    c = lax.axis_index("c")
     tab = lax.axis_index(TAB)
     level_dev, order_count, _, degree_dev = poloidal.shape
     half = order_count // 2
     blocks = half * 2 * degree_dev // 128
-    rad_pair = xl * 16 + z
-    matrix = level_matrix((rad_pair * 2 + c) * level_dev, level_dev)
+    near = lax.axis_index(NEAR)
+    near_count = lax.axis_size(NEAR)
+    far_count = lax.axis_size("zf")
+    matrix = level_matrix(lax.axis_index(RAD) * level_dev, level_dev)
     partial = level_sums(matrix, poloidal, toroidal)
     pair = lax.all_gather(partial, "c", axis=0)
     pair = lax.dynamic_slice_in_dim(pair, c * blocks, blocks, 1).astype(jnp.float32)
     partial = (pair[0] + pair[1]).astype(jnp.bfloat16)
-    shares = lax.all_to_all(partial, ("xl", "z"), 0, 0, tiled=True)
-    radial = jnp.sum(shares.astype(jnp.float32), axis=0).reshape(3, SHELLS, 128)
+    shares = lax.all_to_all(partial, NEAR, 0, 0, tiled=True)
+    shares = shares.reshape(near_count, -1, 3 * SHELLS, 128).astype(jnp.float32)
+    copies = jnp.broadcast_to(
+        jnp.sum(shares, axis=0).astype(jnp.bfloat16), (far_count,) + shares.shape[1:]
+    )
+    shares = lax.all_to_all(copies, "zf", 0, 0, tiled=True)
+    radial = jnp.sum(shares.astype(jnp.float32), axis=0)
+    radial = radial.reshape(2, degree_dev // 128, 3, SHELLS, 128)
 
-    order = orders[c * half + rad_pair // 4]
-    degree = tab * degree_dev + (rad_pair % 2) * 128 + jnp.arange(128, dtype=jnp.int32)
+    order = lax.dynamic_index_in_dim(orders, c * half + near, keepdims=False)
+    degree = tab * degree_dev + jnp.arange(degree_dev, dtype=jnp.int32)
     degree_wide = degree.astype(jnp.float32)
     weight = jnp.where(degree >= order, jnp.sqrt(degree_wide * (degree_wide + 1.0)), 0.0)
-    spheroidal = radial[0] / shell_radius()[:, None]
+    weight = weight.reshape(1, degree_dev // 128, 1, 128)
+    spheroidal = radial[:, :, 0] / shell_radius()[:, None]
     spectra = jnp.stack(
-        [weight * spheroidal, weight * (spheroidal + radial[1]), weight * radial[2]]
+        [
+            weight * spheroidal,
+            weight * (spheroidal + radial[:, :, 1]),
+            weight * radial[:, :, 2],
+        ],
+        axis=2,
     ).astype(jnp.bfloat16)
-    spectra = jnp.broadcast_to(spectra.reshape(1, 3 * SHELLS, 128), (blocks, 3 * SHELLS, 128))
-    spectra = lax.all_to_all(spectra, ("xl", "z"), 0, 0, tiled=True)
+    spectra = jnp.broadcast_to(
+        spectra.reshape(1, -1, 3 * SHELLS, 128), (near_count, blocks // near_count, 3 * SHELLS, 128)
+    )
+    spectra = lax.all_to_all(spectra, NEAR, 0, 0, tiled=True)
     spectra = lax.all_gather(spectra, "c", axis=0, tiled=True)
     coef = spectra.reshape(order_count, 2, 2, 3, SHELLS, 128).transpose(3, 0, 4, 1, 2, 5)
     coef = coef.reshape(3, order_count, SHELLS, 2, degree_dev)
@@ -131,7 +148,7 @@
 
 
 def solution(mesh):
-    fine = Mesh(mesh.devices.reshape(2, 4, 2, 16, 2), TAB + RAD)
+    fine = Mesh(mesh.devices.reshape(2, 4, 2, 4, 4, 2), TAB + RAD)
     placed = (
         P(RAD, None, None, TAB),
         P(RAD, None, None, TAB),

time: 86.4 us -> 80.2 us (0.928)
  waiting for transfers between devices: 37.9 us -> 24.1 us
  blocking collectives: 14.9 us -> 24 us
  starting transfers between devices: 21.5 us -> 20.1 us
    all_to_all x2, waiting for transfers between devices: 31 us -> 17.2 us  [the longest x1 12.1 us: on_device(): shares = lax.all_to_all(copies, 'zf', 0, 0, tiled=True)]
    all_to_all x0 -> x1, blocking collectives: none -> 10.2 us  [on_device(): shares = lax.all_to_all(partial, NEAR, 0, 0, tiled=True)]
    all_to_all x2, starting transfers between devices: 15.1 us -> 13.7 us  [the longest x1 10.4 us: on_device(): shares = lax.all_to_all(copies, 'zf', 0, 0, tiled=True)]
    all_gather x1, blocking collectives: 5.82 us -> 4.73 us  [on_device(): spectra = lax.all_gather(spectra, 'c', axis=0, tiled=True)]
where the time goes in v3:
time: 80.2 us; the launch traced here: 79.8 us
  waiting for transfers between devices  24.1 us (30%)
  blocking collectives  24 us (30%)
  starting transfers between devices  20.1 us (25%)
  other arithmetic  3.82 us (5%)
  local copies, waits for them, and re-layouts  3.08 us (4%)
  matrix products  2.37 us (3%)
  Pallas kernels  2.12 us (3%)
    all_to_all x1, waiting for transfers between devices, on_device(): shares = lax.all_to_all(copies, 'zf', 0, 0, tiled=True)  12.1 us
    all_to_all x1, starting transfers between devices, on_device(): shares = lax.all_to_all(copies, 'zf', 0, 0, tiled=True)  10.4 us
    all_to_all x1, blocking collectives, on_device(): shares = lax.all_to_all(partial, NEAR, 0, 0, tiled=True)  10.2 us
    all_gather x1, blocking collectives, on_device(): pair = lax.all_gather(partial, 'c', axis=0)  9.06 us
    all_to_all x1, waiting for transfers between devices, on_device(): lax.all_to_all(fourier.astype(jnp.bfloat16), TAB, 0, 0, tiled=True)  6.84 us
    all_to_all x1, starting transfers between devices, on_device(): lax.all_to_all(fourier.astype(jnp.bfloat16), TAB, 0, 0, tiled=True)  6.36 us
    all_to_all x1, waiting for transfers between devices, on_device(): spectra = lax.all_to_all(spectra, NEAR, 0, 0, tiled=True)  5.14 us
    all_gather x1, blocking collectives, on_device(): spectra = lax.all_gather(spectra, 'c', axis=0, tiled=True)  4.73 us
  transfers between devices with their start and end apart: 3, of which 3 were waited for; matrix products, arithmetic and copies ran while one was open for 4% of the time, Pallas kernels for 0%

profile of v3, /device:TPU:1, one launch (start us, length us, event | category | flops | bytes accessed | tf_op | source)
XLA Modules:
  0.0 79.8 jit_solution(1511399476064789339)
XLA Ops:
  0.1 0.9 %fusion.44.matrix_ref = bf16[48,128]{1,0:T(8,128)(2,1)} fusion(s32[48]{0:T(128)S(1)} %get-tuple-element.34, s32[48]{0:T(128)S(1)} %get-tuple-element.35, s32[128]{0:T(128)S(1)} %get-tuple-element.29, s32[128]{0:T(128)S(1)} %get-tuple-element.31, s32[]{:T(128)S(6)} %mul.141, s32[128]{0:T(128)S(1)} %get-tuple-element.28, s32[128]{0:T(128)S(1)} %get-tuple-element.36, ...), kind=kLoop, calls=%fused_computation.95 | loop fusion | flops 509952 | bytes 17044 | tf_op jit(solution)/shard_map/convert_element_type | solution.py:37
  1.1 2.1 %level_sums.1 = bf16[64,24,128]{2,1,0:T(8,128)(2,1)} custom-call(bf16[48,128]{1,0:T(8,128)(2,1)} %fusion.44.matrix_ref, bf16[16,16,2,256]{3,2,1,0:T(2,128)(2,1)} %pol_ref.1, bf16[16,16,2,256]{3,2,1,0:T(2,128)(2,1)} %tor_ref.1), custom_call_target="tpu_custom_call" | custom-call | tf_op jit(solution)/shard_map/level_sums/pallas_call | solution.py:56
  3.2 9.1 %all-gather = bf16[128,24,128]{2,1,0:T(8,128)(2,1)S(1)} all-gather(bf16[64,24,128]{2,1,0:T(8,128)(2,1)} %level_sums.1), channel_id=2, replica_groups=mesh['xh'=2,'y'=4,'xl'=2,'zf'=4,'zn'=4,'c'=2] {'c'}, dimensions={0}, use_global_device_ids=true | all-gather | bytes 1179648 | tf_op jit(solution)/shard_map/all_gather | solution.py:93
  12.2 0.0 copy-start.1
  12.2 0.1 dynamic-slice_convert_fusion
  12.3 0.0 copy-start
  12.4 10.2 %all_to_all.20 = bf16[32,24,128]{2,1,0:T(8,128)(2,1)S(1)} all-to-all(bf16[32,24,128]{2,1,0:T(8,128)(2,1)S(1)} %fusion.29), channel_id=1, replica_groups=mesh['xh'=2,'y'=4,'xl'=2,'zf'=4,'zn'=4,'c'=2] {'xl','zn'}, dimensions={0} | all-to-all | bytes 393216 | tf_op jit(solution)/shard_map/all_to_all | solution.py:96
  22.6 0.7 broadcast_in_dim.20
  23.3 10.4 %all-to-all-start.1 = ((bf16[4,4,24,128]{3,2,1,0:T(8,128)(2,1)}), bf16[4,4,24,128]{3,2,1,0:T(8,128)(2,1)S(1)}, u32[]{:S(2)}, u32[]{:S(2)}) async-start(bf16[4,4,24,128]{3,2,1,0:T(8,128)(2,1)} %broadcast_in_dim.20), calls=%async_computation.1 | async-start | bytes 196608 | tf_op jit(solution)/shard_map/all_to_all | solution.py:101
  33.6 0.0 copy-done.1
  33.6 0.6 dynamic_slice.7
  34.3 0.7 compare_select_fusion
  34.9 12.1 %all-to-all-done.1 = bf16[4,4,24,128]{3,2,1,0:T(8,128)(2,1)S(1)} async-done(((bf16[4,4,24,128]{3,2,1,0:T(8,128)(2,1)}), bf16[4,4,24,128]{3,2,1,0:T(8,128)(2,1)S(1)}, u32[]{:S(2)}, u32[]{:S(2)}) %all-to-all-start.1) | async-done | bytes 98336 | tf_op jit(solution)/shard_map/all_to_all | solution.py:101
  47.0 0.1 multiply_convert_fusion
  47.1 0.7 broadcast_in_dim.21
  47.8 3.4 %all-to-all-start.2 = ((bf16[8,4,24,128]{3,2,1,0:T(8,128)(2,1)}), bf16[8,4,24,128]{3,2,1,0:T(8,128)(2,1)S(1)}, u32[]{:S(2)}, u32[]{:S(2)}) async-start(bf16[8,4,24,128]{3,2,1,0:T(8,128)(2,1)} %broadcast_in_dim.21), calls=%async_computation.2 | async-start | bytes 393216 | tf_op jit(solution)/shard_map/all_to_all | solution.py:122
  51.2 1.7 %cosine_multiply_fusion = (f32[16,6144]{1,0:T(8,128)S(1)}, f32[16,6144]{1,0:T(8,128)S(1)}) fusion(s32[16]{0:T(128)S(1)} %copy-done.1), kind=kLoop, calls=%fused_computation.35 | loop fusion | flops 1081344 | bytes 786496 | tf_op jit(solution)/shard_map/mul | solution.py:70
  52.9 0.0 copy-done
  52.9 0.1 slice_bitcast_fusion.1
  53.0 5.1 %all-to-all-done.2 = bf16[8,4,24,128]{3,2,1,0:T(8,128)(2,1)S(1)} async-done(((bf16[8,4,24,128]{3,2,1,0:T(8,128)(2,1)}), bf16[8,4,24,128]{3,2,1,0:T(8,128)(2,1)S(1)}, u32[]{:S(2)}, u32[]{:S(2)}) %all-to-all-start.2) | async-done | bytes 196640 | tf_op jit(solution)/shard_map/all_to_all | solution.py:122
  58.1 4.7 %all_gather.11 = bf16[16,4,24,128]{3,2,1,0:T(8,128)(2,1)S(1)} all-gather(bf16[8,4,24,128]{3,2,1,0:T(8,128)(2,1)S(1)} %all-to-all-done.2), channel_id=1, replica_groups=mesh['xh'=2,'y'=4,'xl'=2,'zf'=4,'zn'=4,'c'=2] {'c'}, dimensions={0}, use_global_device_ids=true | all-gather | bytes 589824 | tf_op jit(solution)/shard_map/all_gather | solution.py:123
  62.9 0.2 fusion.6
  63.2 0.3 fusion.5
  63.6 0.2 copy.10
  63.8 0.8 %convert_element_type.88 = bf16[8,32,144]{2,1,0:T(8,128)(2,1)} reshape(bf16[8,2,16,3,48]{4,3,2,1,0:T(4,128)(2,1)S(1)} %copy.10) | data formatting | bytes 147456 | tf_op jit(solution)/shard_map/convert_element_type | solution.py:137
  64.6 6.4 %all-to-all-start.3 = ((bf16[8,32,144]{2,1,0:T(8,128)(2,1)}), bf16[8,32,144]{2,1,0:T(8,128)(2,1)S(1)}, u32[]{:S(2)}, u32[]{:S(2)}) async-start(bf16[8,32,144]{2,1,0:T(8,128)(2,1)} %convert_element_type.88), calls=%async_computation.3 | async-start | bytes 262144 | tf_op jit(solution)/shard_map/all_to_all | solution.py:137
  70.9 0.1 fusion.7
  71.0 6.8 %all-to-all-done.3 = bf16[8,32,144]{2,1,0:T(8,128)(2,1)S(1)} async-done(((bf16[8,32,144]{2,1,0:T(8,128)(2,1)}), bf16[8,32,144]{2,1,0:T(8,128)(2,1)S(1)}, u32[]{:S(2)}, u32[]{:S(2)}) %all-to-all-start.3) | async-done | bytes 73760 | tf_op jit(solution)/shard_map/all_to_all | solution.py:137
  77.9 1.9 %convolution_convert_fusion = bf16[144,6144]{1,0:T(8,128)(2,1)} fusion(bf16[32,6144]{1,0:T(8,128)(2,1)S(1)} %get-tuple-element.8, bf16[32,6144]{1,0:T(8,128)(2,1)S(1)} %get-tuple-element.7, bf16[32,144]{1,0:T(8,128)(2,1)S(1)} %get-tuple-element.21, bf16[32,144]{1,0:T(8,128)(2,1)S(1)} %get-tuple-element.20), kind=kOutput, calls=%fused_computation | convolution fusion | flops 174375936 | bytes 2574336 | tf_op jit(solution)/shard_map/dot_general | solution.py:141
  (23 shorter events, 0.4 us)
Async XLA Ops:
  12.2 21.4 %copy-start.1 = (s32[16]{0:T(128)S(1)}, s32[16]{0:T(128)}, u32[]{:S(2)}) copy-start(s32[16]{0:T(128)} %param.7) | copy-start | bytes 196
  12.3 40.6 %copy-start = (bf16[3,16,48,256]{3,2,1,0:T(8,128)(2,1)S(1)}, bf16[3,16,48,256]{3,2,1,0:T(8,128)(2,1)}, u32[]{:S(2)}) copy-start(bf16[3,16,48,256]{3,2,1,0:T(8,128)(2,1)} %param.6) | copy-start | bytes 3538948
  23.3 23.7 %all-to-all-start.1 = ((bf16[4,4,24,128]{3,2,1,0:T(8,128)(2,1)}), bf16[4,4,24,128]{3,2,1,0:T(8,128)(2,1)S(1)}, u32[]{:S(2)}, u32[]{:S(2)}) async-start(bf16[4,4,24,128]{3,2,1,0:T(8,128)(2,1)} %broadcast_in_dim.20), calls=%async_computation.1 | async-start | bytes 196608 | tf_op jit(solution)/shard_map/all_to_all | solution.py:101
  47.8 10.3 %all-to-all-start.2 = ((bf16[8,4,24,128]{3,2,1,0:T(8,128)(2,1)}), bf16[8,4,24,128]{3,2,1,0:T(8,128)(2,1)S(1)}, u32[]{:S(2)}, u32[]{:S(2)}) async-start(bf16[8,4,24,128]{3,2,1,0:T(8,128)(2,1)} %broadcast_in_dim.21), calls=%async_computation.2 | async-start | bytes 393216 | tf_op jit(solution)/shard_map/all_to_all | solution.py:122
  64.6 13.3 %all-to-all-start.3 = ((bf16[8,32,144]{2,1,0:T(8,128)(2,1)}), bf16[8,32,144]{2,1,0:T(8,128)(2,1)S(1)}, u32[]{:S(2)}, u32[]{:S(2)}) async-start(bf16[8,32,144]{2,1,0:T(8,128)(2,1)} %convert_element_type.88), calls=%async_computation.3 | async-start | bytes 262144 | tf_op jit(solution)/shard_map/all_to_all | solution.py:137

commit v4 on v3

v4 whole, which is shorter than its diff:
```python
import math

import jax
import jax.numpy as jnp
import numpy as np
from jax import lax
from jax.experimental import pallas as pl
from jax.experimental.pallas import tpu as pltpu
from jax.sharding import Mesh, PartitionSpec as P

NPHI = 6144
SHELLS = 8
RAD = ("xl", "zf", "zn", "c")
NEAR = ("xl", "zn")
TAB = ("xh", "y")


def shell_radius():
    angle = math.pi / (2 * SHELLS) * (2 * np.arange(SHELLS) + 1)
    return (1.04 + 0.5 * np.cos(angle)).astype(np.float32)


def level_constants(level_dev):
    row = np.arange(2 * 3 * SHELLS)[:, None]
    col = np.arange(4 * level_dev * 2)[None, :]
    kind = row % (3 * SHELLS) // SHELLS
    odd = 2 * (row % SHELLS) + 1
    source = col // (2 * level_dev)
    used = (row // (3 * SHELLS) == col % 2) & ((kind < 2) == (source < 2))
    step_angle = math.pi / (2 * SHELLS)
    planes = []
    for parity in range(4 * SHELLS // level_dev):
        level = parity * level_dev + col % (2 * level_dev) // 2
        angle = step_angle * (level * odd % (4 * SHELLS))
        value = np.where(used & (kind != 1), np.cos(angle), 0.0)
        slope = np.where(used & (kind == 1), 2.0 * np.sin(angle) / np.sin(step_angle * odd), 0.0)
        planes.append(np.stack([value, slope]))
    return np.stack(planes).astype(np.float32)


def level_kernel(constant_ref, pol_ref, tor_ref, out_ref):
    level_dev, order_count, _, degree_dev = pol_ref.shape
    rows = out_ref.shape[1]
    run = lax.axis_index(RAD)
    plane = lax.rem(run, constant_ref.shape[0])
    col = lax.broadcasted_iota(jnp.int32, constant_ref.shape[2:], 1)
    level = (run * level_dev + col % (2 * level_dev) // 2).astype(jnp.float32)
    entry = constant_ref[plane, 0] + level * constant_ref[plane, 1]
    high = entry.astype(jnp.bfloat16)
    low = (entry - high.astype(jnp.float32)).astype(jnp.bfloat16)
    matrix = jnp.where(col // (2 * level_dev) % 2 == 0, high, low)
    for order in range(order_count):
        pol = pol_ref[:, order].reshape(2 * level_dev, degree_dev)
        tor = tor_ref[:, order].reshape(2 * level_dev, degree_dev)
        sums = dot32(matrix, jnp.concatenate([pol, pol, tor, tor], axis=0))
        for part in range(2):
            for cut in range(degree_dev // 128):
                block = sums[part * rows : (part + 1) * rows, cut * 128 : (cut + 1) * 128]
                out_ref[(order * 2 + part) * (degree_dev // 128) + cut] = block.astype(jnp.bfloat16)


def level_sums(poloidal, toroidal):
    level_dev, order_count, _, degree_dev = poloidal.shape
    return pl.pallas_call(
        level_kernel,
        out_shape=jax.ShapeDtypeStruct(
            (order_count * 2 * degree_dev // 128, 3 * SHELLS, 128), jnp.bfloat16
        ),
        compiler_params=pltpu.CompilerParams(vmem_limit_bytes=60 << 20),
        name="level_sums",
    )(level_constants(level_dev), poloidal, toroidal)


def longitude_table(orders, points):
    positions = jnp.arange(points, dtype=jnp.int32)
    turn_counts = orders[:, None] * positions[None, :] % points
    angles = 2.0 * math.pi / points * turn_counts.astype(jnp.float32)
    return jnp.concatenate([2.0 * jnp.cos(angles), -2.0 * jnp.sin(angles)], axis=0)


def split_bf16(x):
    hi = lax.reduce_precision(x, 8, 7)
    return hi.astype(jnp.bfloat16), (x - hi).astype(jnp.bfloat16)


def dot32(a, b):
    return jnp.dot(a, b, preferred_element_type=jnp.float32)


def on_device(poloidal, toroidal, tables, orders):
    c = lax.axis_index("c")
    tab = lax.axis_index(TAB)
    _, order_count, _, degree_dev = poloidal.shape
    half = order_count // 2
    blocks = half * 2 * degree_dev // 128
    near = lax.axis_index(NEAR)
    near_count = lax.axis_size(NEAR)
    far_count = lax.axis_size("zf")
    own_order = c * half + near
    first_degree = tab * degree_dev
    first_block = c * blocks
    partial = level_sums(poloidal, toroidal)
    partial, own_order, first_degree, first_block = lax.optimization_barrier(
        (partial, own_order, first_degree, first_block)
    )
    pair = lax.all_gather(partial, "c", axis=0)
    pair = lax.dynamic_slice_in_dim(pair, first_block, blocks, 1).astype(jnp.float32)
    partial = (pair[0] + pair[1]).astype(jnp.bfloat16)
    shares = lax.all_to_all(partial, NEAR, 0, 0, tiled=True)
    shares = shares.reshape(near_count, -1, 3 * SHELLS, 128).astype(jnp.float32)
    near_sum = lax.optimization_barrier(jnp.sum(shares, axis=0))
    copies = jnp.broadcast_to(near_sum.astype(jnp.bfloat16), (far_count,) + near_sum.shape)
    copies, orders, tables = lax.optimization_barrier((copies, orders, tables))
    shares = lax.all_to_all(copies, "zf", 0, 0, tiled=True)
    order = jnp.sum(jnp.where(jnp.arange(order_count) == own_order, orders, 0))
    degree = first_degree + jnp.arange(degree_dev, dtype=jnp.int32)
    degree_wide = degree.astype(jnp.float32)
    weight = jnp.where(degree >= order, jnp.sqrt(degree_wide * (degree_wide + 1.0)), 0.0)
    weight = weight.reshape(1, degree_dev // 128, 1, 128)
    p_hi, p_lo = split_bf16(longitude_table(orders, NPHI))
    pair_table = jnp.concatenate([tables[1], tables[2]], axis=-1)
    shares, weight, p_hi, p_lo, plain_table, pair_table = lax.optimization_barrier(
        (shares, weight, p_hi, p_lo, tables[0], pair_table)
    )
    radial = jnp.sum(shares.astype(jnp.float32), axis=0)
    radial = radial.reshape(2, degree_dev // 128, 3, SHELLS, 128)
    spheroidal = radial[:, :, 0] / shell_radius()[:, None]
    spectra = jnp.stack(
        [
            weight * spheroidal,
            weight * (spheroidal + radial[:, :, 1]),
            weight * radial[:, :, 2],
        ],
        axis=2,
    ).astype(jnp.bfloat16)
    spectra = jnp.broadcast_to(
        spectra.reshape(1, -1, 3 * SHELLS, 128), (near_count, blocks // near_count, 3 * SHELLS, 128)
    )
    spectra = lax.all_to_all(spectra, NEAR, 0, 0, tiled=True)
    spectra = lax.all_gather(spectra, "c", axis=0, tiled=True)
    coef = spectra.reshape(order_count, 2, 2, 3, SHELLS, 128).transpose(3, 0, 4, 1, 2, 5)
    coef = coef.reshape(3, order_count, SHELLS, 2, degree_dev)

    q, s, t = coef[0], coef[1], coef[2]
    swap = lambda v: jnp.stack([-v[:, :, 1], v[:, :, 0]], axis=2)
    theta = jnp.concatenate([s, swap(t)], axis=-1)
    phi = jnp.concatenate([-t, swap(s)], axis=-1)
    both = jnp.concatenate([theta, phi], axis=1)
    plain = jnp.einsum("mscl,mal->mcsa", q, plain_table, preferred_element_type=jnp.float32)
    pair = jnp.einsum("mscl,mal->mcsa", both, pair_table, preferred_element_type=jnp.float32)
    fourier = jnp.stack([plain, pair[:, :, :SHELLS], pair[:, :, SHELLS:]])
    fourier = fourier.transpose(3, 2, 1, 0, 4).reshape(SHELLS, 2 * order_count, -1)
    fourier = lax.all_to_all(fourier.astype(jnp.bfloat16), TAB, 0, 0, tiled=True)
    summed = jnp.sum(fourier.astype(jnp.float32), axis=0)
    f_hi, f_lo = split_bf16(summed)
    values = lax.dot_general(
        jnp.concatenate([f_hi, f_hi, f_lo]),
        jnp.concatenate([p_hi, p_lo, p_hi]),
        (((0,), (0,)), ((), ())),
        preferred_element_type=jnp.float32,
    )
    return values.astype(jnp.bfloat16).reshape(3, 1, -1, NPHI)


def solution(mesh):
    fine = Mesh(mesh.devices.reshape(2, 4, 2, 4, 4, 2), TAB + RAD)
    placed = (
        P(RAD, None, None, TAB),
        P(RAD, None, None, TAB),
        P(None, None, RAD, TAB),
        P(),
    )
    return jax.shard_map(
        on_device,
        mesh=fine,
        in_specs=placed,
        out_specs=P(None, TAB, RAD, None),
        check_vma=False,
    )
```

time: 80.2 us -> 77.3 us (0.964)
  blocking collectives: 24 us -> 47.2 us
  waiting for transfers between devices: 24.1 us -> 10.1 us
  starting transfers between devices: 20.1 us -> 10.4 us
  local copies, waits for them, and re-layouts: 3.08 us -> 1.17 us
    all_to_all x0 -> x2, blocking collectives: none -> 22.4 us  [the longest x1 13.1 us: on_device(): lax.all_to_all(fourier.astype(jnp.bfloat16), TAB, 0, 0, tiled=True)]
    all_to_all x2 -> x0, waiting for transfers between devices: 12 us -> none  [the longest x1 6.84 us: on_device(): lax.all_to_all(fourier.astype(jnp.bfloat16), TAB, 0, 0, tiled=True)]
    all_to_all x2 -> x0, starting transfers between devices: 9.75 us -> none  [the longest x1 6.36 us: on_device(): lax.all_to_all(fourier.astype(jnp.bfloat16), TAB, 0, 0, tiled=True)]
    all_to_all x1, waiting for transfers between devices: 12.1 us -> 10.1 us  [on_device(): shares = lax.all_to_all(copies, 'zf', 0, 0, tiled=True)]
    convert_element_type x2 -> x1, other arithmetic: 0.97 us -> 0.05 us  [on_device(): lax.dynamic_slice_in_dim(pair, first_block, blocks, 1).astype(jnp.float32)]
  transfers between devices with their start and end apart: 3 -> 1, of which waited for: 3 -> 1; matrix products, arithmetic and copies ran while one was open for 4% -> 4% of each run, Pallas kernels for 0% -> 0%
where the time goes in v4:
time: 77.3 us; the launch traced here: 77 us
  blocking collectives  47.2 us (61%)
  starting transfers between devices  10.4 us (13%)
  waiting for transfers between devices  10.1 us (13%)
  other arithmetic  3.51 us (5%)
  matrix products  2.38 us (3%)
  Pallas kernels  2.16 us (3%)
  local copies, waits for them, and re-layouts  1.17 us (2%)
    all_to_all x1, blocking collectives, on_device(): lax.all_to_all(fourier.astype(jnp.bfloat16), TAB, 0, 0, tiled=True)  13.1 us
    all_to_all x1, starting transfers between devices, on_device(): shares = lax.all_to_all(copies, 'zf', 0, 0, tiled=True)  10.4 us
    all_to_all x1, blocking collectives, on_device(): shares = lax.all_to_all(partial, NEAR, 0, 0, tiled=True)  10.2 us
    all_to_all x1, waiting for transfers between devices, on_device(): shares = lax.all_to_all(copies, 'zf', 0, 0, tiled=True)  10.1 us
    all_to_all x1, blocking collectives, on_device(): spectra = lax.all_to_all(spectra, NEAR, 0, 0, tiled=True)  9.32 us
    all_gather x1, blocking collectives, on_device(): pair = lax.all_gather(partial, 'c', axis=0)  9.07 us
    all_gather x1, blocking collectives, on_device(): spectra = lax.all_gather(spectra, 'c', axis=0, tiled=True)  5.49 us
    pallas_call x1, Pallas kernels, level_sums(): pl.pallas_call(level_kernel, out_shape=jax.ShapeDtypeStruct((order_count...  2.16 us
  transfers between devices with their start and end apart: 1, of which 1 were waited for; matrix products, arithmetic and copies ran while one was open for 4% of the time, Pallas kernels for 0%

profile of v4, /device:TPU:1, one launch (start us, length us, event | category | flops | bytes accessed | tf_op | source)
XLA Modules:
  0.0 77.0 jit_solution(7957707719409468355)
XLA Ops:
  0.0 2.2 %level_sums.1 = bf16[64,24,128]{2,1,0:T(8,128)(2,1)} custom-call(f32[2,2,48,128]{3,2,1,0:T(8,128)} %constant.61.clone.constant_ref, bf16[16,16,2,256]{3,2,1,0:T(2,128)(2,1)} %pol_ref.1, bf16[16,16,2,256]{3,2,1,0:T(2,128)(2,1)} %tor_ref.1), custom_call_target="tpu_custom_call" | custom-call | tf_op jit(solution)/shard_map/level_sums/pallas_call | solution.py:64
  2.2 9.1 %all-gather = bf16[128,24,128]{2,1,0:T(8,128)(2,1)S(1)} all-gather(bf16[64,24,128]{2,1,0:T(8,128)(2,1)} %level_sums.1), channel_id=2, replica_groups=mesh['xh'=2,'y'=4,'xl'=2,'zf'=4,'zn'=4,'c'=2] {'c'}, dimensions={0}, use_global_device_ids=true | all-gather | bytes 1179648 | tf_op jit(solution)/shard_map/all_gather | solution.py:106
  11.2 0.0 copy-start.2
  11.2 0.1 dynamic-slice_convert_fusion
  11.3 0.0 copy-start
  11.4 10.2 %all_to_all.20 = bf16[32,24,128]{2,1,0:T(8,128)(2,1)S(1)} all-to-all(bf16[32,24,128]{2,1,0:T(8,128)(2,1)S(1)} %fusion.27), channel_id=1, replica_groups=mesh['xh'=2,'y'=4,'xl'=2,'zf'=4,'zn'=4,'c'=2] {'xl','zn'}, dimensions={0} | all-to-all | bytes 393216 | tf_op jit(solution)/shard_map/all_to_all | solution.py:109
  21.6 0.7 broadcast_in_dim.19
  22.2 10.4 %all-to-all-start.1 = ((bf16[4,4,24,128]{3,2,1,0:T(8,128)(2,1)}), bf16[4,4,24,128]{3,2,1,0:T(8,128)(2,1)S(1)}, u32[]{:S(2)}, u32[]{:S(2)}) async-start(bf16[4,4,24,128]{3,2,1,0:T(8,128)(2,1)} %broadcast_in_dim.19), calls=%async_computation.1 | async-start | bytes 196608 | tf_op jit(solution)/shard_map/all_to_all | solution.py:114
  32.6 0.0 copy-done.2
  32.6 1.7 %cosine_multiply_fusion = (f32[16,6144]{1,0:T(8,128)S(1)}, f32[16,6144]{1,0:T(8,128)S(1)}) fusion(s32[16]{0:T(128)S(1)} %copy-done.2), kind=kLoop, calls=%fused_computation.38 | loop fusion | flops 1081344 | bytes 786496 | tf_op jit(solution)/shard_map/mul | solution.py:78
  34.3 0.0 copy-done
  34.3 0.1 slice_bitcast_fusion.1
  34.4 0.0 copy-start.1
  34.4 0.1 fusion.7
  34.5 0.7 fusion.38
  35.2 0.6 compare_select_fusion
  35.8 0.1 pad_maximum_fusion.1
  35.9 10.1 %all-to-all-done.1 = bf16[4,4,24,128]{3,2,1,0:T(8,128)(2,1)S(1)} async-done(((bf16[4,4,24,128]{3,2,1,0:T(8,128)(2,1)}), bf16[4,4,24,128]{3,2,1,0:T(8,128)(2,1)S(1)}, u32[]{:S(2)}, u32[]{:S(2)}) %all-to-all-start.1) | async-done | bytes 98336 | tf_op jit(solution)/shard_map/all_to_all | solution.py:114
  46.0 0.0 copy-done.1
  46.0 0.1 multiply_convert_fusion
  46.1 9.3 %all_to_all.21 = bf16[8,4,24,128]{3,2,1,0:T(8,128)(2,1)S(1)} all-to-all(bf16[8,4,24,128]{3,2,1,0:T(8,128)(2,1)S(1)} %broadcast_in_dim.22), channel_id=1, replica_groups=mesh['xh'=2,'y'=4,'xl'=2,'zf'=4,'zn'=4,'c'=2] {'xl','zn'}, dimensions={0} | all-to-all | bytes 393216 | tf_op jit(solution)/shard_map/all_to_all | solution.py:139
  55.5 5.5 %all_gather.11 = bf16[16,4,24,128]{3,2,1,0:T(8,128)(2,1)S(1)} all-gather(bf16[8,4,24,128]{3,2,1,0:T(8,128)(2,1)S(1)} %all_to_all.21), channel_id=1, replica_groups=mesh['xh'=2,'y'=4,'xl'=2,'zf'=4,'zn'=4,'c'=2] {'c'}, dimensions={0}, use_global_device_ids=true | all-gather | bytes 589824 | tf_op jit(solution)/shard_map/all_gather | solution.py:140
  61.0 0.2 fusion.6
  61.2 0.3 fusion.5
  61.6 0.1 maximum_bitcast_fusion
  61.7 0.2 copy.12
  61.9 0.2 convert_element_type.80
  62.0 13.1 %all_to_all.22 = bf16[8,32,144]{2,1,0:T(8,128)(2,1)S(1)} all-to-all(bf16[8,32,144]{2,1,0:T(8,128)(2,1)S(1)} %convert_element_type.80), channel_id=1, replica_groups=mesh['xh'=2,'y'=4,'xl'=2,'zf'=4,'zn'=4,'c'=2] {'xh','y'}, dimensions={0} | all-to-all | bytes 147456 | tf_op jit(solution)/shard_map/all_to_all | solution.py:153
  75.1 1.9 %convolution_convert_fusion = bf16[144,6144]{1,0:T(8,128)(2,1)} fusion(bf16[32,6144]{1,0:T(8,128)(2,1)S(1)} %get-tuple-element.29, bf16[32,6144]{1,0:T(8,128)(2,1)S(1)} %get-tuple-element.30, bf16[32,144]{1,0:T(8,128)(2,1)S(1)} %get-tuple-element.48, bf16[32,144]{1,0:T(8,128)(2,1)S(1)} %get-tuple-element.47), kind=kOutput, calls=%fused_computation | convolution fusion | flops 174375936 | bytes 2574336 | tf_op jit(solution)/shard_map/dot_general | solution.py:156
  (11 shorter events, 0.3 us)
Async XLA Ops:
  11.2 21.4 %copy-start.2 = (s32[16]{0:T(128)S(1)}, s32[16]{0:T(128)}, u32[]{:S(2)}) copy-start(s32[16]{0:T(128)} %param.9) | copy-start | bytes 196
  11.3 23.0 %copy-start = (bf16[3,16,48,256]{3,2,1,0:T(8,128)(2,1)S(1)}, bf16[3,16,48,256]{3,2,1,0:T(8,128)(2,1)}, u32[]{:S(2)}) copy-start(bf16[3,16,48,256]{3,2,1,0:T(8,128)(2,1)} %param.8) | copy-start | bytes 3538948
  22.2 23.7 %all-to-all-start.1 = ((bf16[4,4,24,128]{3,2,1,0:T(8,128)(2,1)}), bf16[4,4,24,128]{3,2,1,0:T(8,128)(2,1)S(1)}, u32[]{:S(2)}, u32[]{:S(2)}) async-start(bf16[4,4,24,128]{3,2,1,0:T(8,128)(2,1)} %broadcast_in_dim.19), calls=%async_computation.1 | async-start | bytes 196608 | tf_op jit(solution)/shard_map/all_to_all | solution.py:114
  34.4 11.6 %copy-start.1 = (f32[8]{0:T(128)S(1)}, f32[8]{0:T(128)}, u32[]{:S(2)}) copy-start(f32[8]{0:T(128)} %constant.67) | copy-start | bytes 100

commit v5 on v4

--- a/solution.py
+++ b/solution.py
@@ -12,11 +12,14 @@
 SHELLS = 8
 RAD = ("xl", "zf", "zn", "c")
 NEAR = ("xl", "zn")
+NEAR_ORDER = (5, 6, 7, 4, 1, 2, 3, 0)
+FAR_ORDER = (2, 3, 0, 1)
+TAB_ORDER = (7, 6, 5, 4, 3, 2, 1, 0)
 TAB = ("xh", "y")
 
 
 def shell_radius():
-    angle = math.pi / (2 * SHELLS) * (2 * np.arange(SHELLS) + 1)
+    angle = math.pi / (2 * SHELLS) * (2 * np.array(TAB_ORDER) + 1)
     return (1.04 + 0.5 * np.cos(angle)).astype(np.float32)
 
 
@@ -24,7 +27,7 @@
     row = np.arange(2 * 3 * SHELLS)[:, None]
     col = np.arange(4 * level_dev * 2)[None, :]
     kind = row % (3 * SHELLS) // SHELLS
-    odd = 2 * (row % SHELLS) + 1
+    odd = 2 * np.array(TAB_ORDER)[row % SHELLS] + 1
     source = col // (2 * level_dev)
     used = (row // (3 * SHELLS) == col % 2) & ((kind < 2) == (source < 2))
     step_angle = math.pi / (2 * SHELLS)
@@ -93,7 +96,7 @@
     _, order_count, _, degree_dev = poloidal.shape
     half = order_count // 2
     blocks = half * 2 * degree_dev // 128
-    near = lax.axis_index(NEAR)
+    near = (1 - lax.axis_index("xl")) * 4 + (lax.axis_index("zn") + 3) % 4
     near_count = lax.axis_size(NEAR)
     far_count = lax.axis_size("zf")
     own_order = c * half + near
@@ -106,12 +109,12 @@
     pair = lax.all_gather(partial, "c", axis=0)
     pair = lax.dynamic_slice_in_dim(pair, first_block, blocks, 1).astype(jnp.float32)
     partial = (pair[0] + pair[1]).astype(jnp.bfloat16)
-    shares = lax.all_to_all(partial, NEAR, 0, 0, tiled=True)
+    shares = lax.all_to_all(partial, NEAR, 0, 0, axis_index_groups=[NEAR_ORDER], tiled=True)
     shares = shares.reshape(near_count, -1, 3 * SHELLS, 128).astype(jnp.float32)
     near_sum = lax.optimization_barrier(jnp.sum(shares, axis=0))
     copies = jnp.broadcast_to(near_sum.astype(jnp.bfloat16), (far_count,) + near_sum.shape)
     copies, orders, tables = lax.optimization_barrier((copies, orders, tables))
-    shares = lax.all_to_all(copies, "zf", 0, 0, tiled=True)
+    shares = lax.all_to_all(copies, "zf", 0, 0, axis_index_groups=[FAR_ORDER], tiled=True)
     order = jnp.sum(jnp.where(jnp.arange(order_count) == own_order, orders, 0))
     degree = first_degree + jnp.arange(degree_dev, dtype=jnp.int32)
     degree_wide = degree.astype(jnp.float32)
@@ -136,7 +139,7 @@
     spectra = jnp.broadcast_to(
         spectra.reshape(1, -1, 3 * SHELLS, 128), (near_count, blocks // near_count, 3 * SHELLS, 128)
     )
-    spectra = lax.all_to_all(spectra, NEAR, 0, 0, tiled=True)
+    spectra = lax.all_to_all(spectra, NEAR, 0, 0, axis_index_groups=[NEAR_ORDER], tiled=True)
     spectra = lax.all_gather(spectra, "c", axis=0, tiled=True)
     coef = spectra.reshape(order_count, 2, 2, 3, SHELLS, 128).transpose(3, 0, 4, 1, 2, 5)
     coef = coef.reshape(3, order_count, SHELLS, 2, degree_dev)
@@ -150,7 +153,9 @@
     pair = jnp.einsum("mscl,mal->mcsa", both, pair_table, preferred_element_type=jnp.float32)
     fourier = jnp.stack([plain, pair[:, :, :SHELLS], pair[:, :, SHELLS:]])
     fourier = fourier.transpose(3, 2, 1, 0, 4).reshape(SHELLS, 2 * order_count, -1)
-    fourier = lax.all_to_all(fourier.astype(jnp.bfloat16), TAB, 0, 0, tiled=True)
+    fourier = lax.all_to_all(
+        fourier.astype(jnp.bfloat16), TAB, 0, 0, axis_index_groups=[TAB_ORDER], tiled=True
+    )
     summed = jnp.sum(fourier.astype(jnp.float32), axis=0)
     f_hi, f_lo = split_bf16(summed)
     values = lax.dot_general(

time: 77.3 us -> 64.9 us (0.84)
  waiting for transfers between devices: 10.1 us -> 0.01 us
  blocking collectives: 47.2 us -> 43.2 us
  starting transfers between devices: 10.4 us -> 12 us
    all_to_all x1, waiting for transfers between devices: 10.1 us -> 0.01 us  [on_device(): lax.all_to_all(copies, 'zf', 0, 0, axis_index_groups=[FAR_ORDER], tiled=T...]
    all_to_all x3, blocking collectives: 32.6 us -> 28.3 us  [the longest x1 10.9 us: on_device(): lax.all_to_all(fourier.astype(jnp.bfloat16), TAB, 0, 0, axis_index_groups...]
    all_to_all x1, starting transfers between devices: 10.4 us -> 12 us  [on_device(): lax.all_to_all(copies, 'zf', 0, 0, axis_index_groups=[FAR_ORDER], tiled=T...]
  transfers between devices with their start and end apart: 1 -> 1, of which waited for: 1 -> 0; matrix products, arithmetic and copies ran while one was open for 4% -> 5% of each run, Pallas kernels for 0% -> 0%
where the time goes in v5:
time: 64.9 us; the launch traced here: 64.6 us
  blocking collectives  43.2 us (67%)
  starting transfers between devices  12 us (18%)
  other arithmetic  3.51 us (5%)
  matrix products  2.39 us (4%)
  Pallas kernels  2.16 us (3%)
  local copies, waits for them, and re-layouts  1.17 us (2%)
    all_to_all x1, starting transfers between devices, on_device(): lax.all_to_all(copies, 'zf', 0, 0, axis_index_groups=[FAR_ORDER], tiled=T...  12 us
    all_to_all x1, blocking collectives, on_device(): lax.all_to_all(fourier.astype(jnp.bfloat16), TAB, 0, 0, axis_index_groups...  10.9 us
    all_to_all x1, blocking collectives, on_device(): lax.all_to_all(partial, NEAR, 0, 0, axis_index_groups=[NEAR_ORDER], tiled...  9.13 us
    all_gather x1, blocking collectives, on_device(): pair = lax.all_gather(partial, 'c', axis=0)  9.07 us
    all_to_all x1, blocking collectives, on_device(): lax.all_to_all(spectra, NEAR, 0, 0, axis_index_groups=[NEAR_ORDER], tiled...  8.25 us
    all_gather x1, blocking collectives, on_device(): spectra = lax.all_gather(spectra, 'c', axis=0, tiled=True)  5.83 us
    pallas_call x1, Pallas kernels, level_sums(): pl.pallas_call(level_kernel, out_shape=jax.ShapeDtypeStruct((order_count...  2.16 us
    dot_general x1, matrix products, on_device(): lax.dot_general(jnp.concatenate([f_hi, f_hi, f_lo]), jnp.concatenate([p_h...  1.85 us
  transfers between devices with their start and end apart: 1, of which 0 were waited for; matrix products, arithmetic and copies ran while one was open for 5% of the time, Pallas kernels for 0%

profile of v5, /device:TPU:1, one launch (start us, length us, event | category | flops | bytes accessed | tf_op | source)
XLA Modules:
  0.0 64.6 jit_solution(12481852073395289397)
XLA Ops:
  0.0 2.2 %level_sums.1 = bf16[64,24,128]{2,1,0:T(8,128)(2,1)} custom-call(f32[2,2,48,128]{3,2,1,0:T(8,128)} %constant.74.clone.constant_ref, bf16[16,16,2,256]{3,2,1,0:T(2,128)(2,1)} %pol_ref.1, bf16[16,16,2,256]{3,2,1,0:T(2,128)(2,1)} %tor_ref.1), custom_call_target="tpu_custom_call" | custom-call | tf_op jit(solution)/shard_map/level_sums/pallas_call | solution.py:67
  2.2 9.1 %all-gather = bf16[128,24,128]{2,1,0:T(8,128)(2,1)S(1)} all-gather(bf16[64,24,128]{2,1,0:T(8,128)(2,1)} %level_sums.1), channel_id=2, replica_groups=mesh['xh'=2,'y'=4,'xl'=2,'zf'=4,'zn'=4,'c'=2] {'c'}, dimensions={0}, use_global_device_ids=true | all-gather | bytes 1179648 | tf_op jit(solution)/shard_map/all_gather | solution.py:109
  11.2 0.0 copy-start.2
  11.2 0.1 dynamic-slice_convert_fusion
  11.3 0.0 copy-start
  11.4 9.1 %all_to_all.20 = bf16[32,24,128]{2,1,0:T(8,128)(2,1)S(1)} all-to-all(bf16[32,24,128]{2,1,0:T(8,128)(2,1)S(1)} %fusion.27), channel_id=1, replica_groups={{34,36,38,32,2,4,6,0},{35,37,39,33,3,5,7,1},{42,44,46,40,10,12,14,8},{4..., dimensions={0} | all-to-all | bytes 393216 | tf_op jit(solution)/shard_map/all_to_all | solution.py:112
  20.5 0.7 %broadcast_in_dim.19 = bf16[4,4,24,128]{3,2,1,0:T(8,128)(2,1)} broadcast(bf16[4,24,128]{2,1,0:T(8,128)(2,1)S(1)} %convert_reduce_fusion), dimensions={1,2,3} | broadcast | bytes 122880 | tf_op jit(solution)/shard_map/broadcast_in_dim | solution.py:115
  21.2 12.0 %all-to-all-start.1 = ((bf16[4,4,24,128]{3,2,1,0:T(8,128)(2,1)}), bf16[4,4,24,128]{3,2,1,0:T(8,128)(2,1)S(1)}, u32[]{:S(2)}, u32[]{:S(2)}) async-start(bf16[4,4,24,128]{3,2,1,0:T(8,128)(2,1)} %broadcast_in_dim.19), calls=%async_computation.1 | async-start | bytes 196608 | tf_op jit(solution)/shard_map/all_to_all | solution.py:117
  33.2 0.0 copy-done.2
  33.2 1.7 %cosine_multiply_fusion = (f32[16,6144]{1,0:T(8,128)S(1)}, f32[16,6144]{1,0:T(8,128)S(1)}) fusion(s32[16]{0:T(128)S(1)} %copy-done.2), kind=kLoop, calls=%fused_computation.38 | loop fusion | flops 1081344 | bytes 786496 | tf_op jit(solution)/shard_map/mul | solution.py:81
  34.9 0.0 copy-done
  34.9 0.1 slice_bitcast_fusion.1
  35.0 0.0 copy-start.1
  35.0 0.1 fusion.7
  35.1 0.7 %fusion.38 = s32[]{:T(128)} fusion(s32[16]{0:T(128)S(1)} %copy-done.2, s32[]{:T(128)S(6)} %add.70), kind=kLoop, calls=%fused_computation.75 | loop fusion | flops 47 | bytes 72 | tf_op jit(solution)/shard_map/reduce_sum | solution.py:118
  35.7 0.6 compare_select_fusion
  36.4 0.1 pad_maximum_fusion.1
  36.5 0.0 all-to-all-done.1
  36.5 0.0 copy-done.1
  36.5 0.1 multiply_convert_fusion
  36.6 8.3 %all_to_all.21 = bf16[8,4,24,128]{3,2,1,0:T(8,128)(2,1)S(1)} all-to-all(bf16[8,4,24,128]{3,2,1,0:T(8,128)(2,1)S(1)} %broadcast_in_dim.22), channel_id=1, replica_groups={{34,36,38,32,2,4,6,0},{35,37,39,33,3,5,7,1},{42,44,46,40,10,12,14,8},{4..., dimensions={0} | all-to-all | bytes 393216 | tf_op jit(solution)/shard_map/all_to_all | solution.py:142
  44.9 5.8 %all_gather.11 = bf16[16,4,24,128]{3,2,1,0:T(8,128)(2,1)S(1)} all-gather(bf16[8,4,24,128]{3,2,1,0:T(8,128)(2,1)S(1)} %all_to_all.21), channel_id=1, replica_groups=mesh['xh'=2,'y'=4,'xl'=2,'zf'=4,'zn'=4,'c'=2] {'c'}, dimensions={0}, use_global_device_ids=true | all-gather | bytes 589824 | tf_op jit(solution)/shard_map/all_gather | solution.py:143
  50.8 0.2 fusion.6
  51.0 0.3 fusion.5
  51.4 0.1 maximum_bitcast_fusion
  51.4 0.2 copy.12
  51.6 0.2 convert_element_type.80
  51.8 10.9 %all_to_all.22 = bf16[8,32,144]{2,1,0:T(8,128)(2,1)S(1)} all-to-all(bf16[8,32,144]{2,1,0:T(8,128)(2,1)S(1)} %convert_element_type.80), channel_id=1, replica_groups={{448,384,320,256,192,128,64,0},{449,385,321,257,193,129,65,1},{450,386,..., dimensions={0} | all-to-all | bytes 147456 | tf_op jit(solution)/shard_map/all_to_all | solution.py:156
  62.7 1.9 %convolution_convert_fusion = bf16[144,6144]{1,0:T(8,128)(2,1)} fusion(bf16[32,6144]{1,0:T(8,128)(2,1)S(1)} %get-tuple-element.29, bf16[32,6144]{1,0:T(8,128)(2,1)S(1)} %get-tuple-element.30, bf16[32,144]{1,0:T(8,128)(2,1)S(1)} %get-tuple-element.48, bf16[32,144]{1,0:T(8,128)(2,1)S(1)} %get-tuple-element.47), kind=kOutput, calls=%fused_computation | convolution fusion | flops 174375936 | bytes 2574336 | tf_op jit(solution)/shard_map/dot_general | solution.py:161
  (11 shorter events, 0.3 us)
Async XLA Ops:
  11.2 22.0 %copy-start.2 = (s32[16]{0:T(128)S(1)}, s32[16]{0:T(128)}, u32[]{:S(2)}) copy-start(s32[16]{0:T(128)} %param.9) | copy-start | bytes 196
  11.3 23.6 %copy-start = (bf16[3,16,48,256]{3,2,1,0:T(8,128)(2,1)S(1)}, bf16[3,16,48,256]{3,2,1,0:T(8,128)(2,1)}, u32[]{:S(2)}) copy-start(bf16[3,16,48,256]{3,2,1,0:T(8,128)(2,1)} %param.8) | copy-start | bytes 3538948
  21.2 15.3 %all-to-all-start.1 = ((bf16[4,4,24,128]{3,2,1,0:T(8,128)(2,1)}), bf16[4,4,24,128]{3,2,1,0:T(8,128)(2,1)S(1)}, u32[]{:S(2)}, u32[]{:S(2)}) async-start(bf16[4,4,24,128]{3,2,1,0:T(8,128)(2,1)} %broadcast_in_dim.19), calls=%async_computation.1 | async-start | bytes 196608 | tf_op jit(solution)/shard_map/all_to_all | solution.py:117
  35.0 1.5 %copy-start.1 = (f32[8]{0:T(128)S(1)}, f32[8]{0:T(128)}, u32[]{:S(2)}) copy-start(f32[8]{0:T(128)} %constant.80) | copy-start | bytes 100

commit v6 on v5

--- a/solution.py
+++ b/solution.py
@@ -41,7 +41,29 @@
     return np.stack(planes).astype(np.float32)
 
 
-def level_kernel(constant_ref, pol_ref, tor_ref, out_ref):
+def level_kernel(
+    constant_hbm, pol_hbm, tor_hbm, orders_hbm, out_ref, phase_ref, weight_ref,
+    constant_ref, pol_ref, tor_ref, orders_ref, sems,
+):
+    loads = [
+        pltpu.make_async_copy(source, target, sems.at[at])
+        for at, (source, target) in enumerate(
+            [
+                (orders_hbm, orders_ref),
+                (constant_hbm, constant_ref),
+                (pol_hbm, pol_ref),
+                (tor_hbm, tor_ref),
+            ]
+        )
+    ]
+    for load in loads:
+        load.start()
+    loads[0].wait()
+    weight_rows(orders_ref, weight_ref)
+    longitude_rows(orders_ref, phase_ref)
+    for load in loads[1:]:
+        load.wait()
+
     level_dev, order_count, _, degree_dev = pol_ref.shape
     rows = out_ref.shape[1]
     run = lax.axis_index(RAD)
@@ -49,8 +71,7 @@
     col = lax.broadcasted_iota(jnp.int32, constant_ref.shape[2:], 1)
     level = (run * level_dev + col % (2 * level_dev) // 2).astype(jnp.float32)
     entry = constant_ref[plane, 0] + level * constant_ref[plane, 1]
-    high = entry.astype(jnp.bfloat16)
-    low = (entry - high.astype(jnp.float32)).astype(jnp.bfloat16)
+    high, low = halves(entry)
     matrix = jnp.where(col // (2 * level_dev) % 2 == 0, high, low)
     for order in range(order_count):
         pol = pol_ref[:, order].reshape(2 * level_dev, degree_dev)
@@ -62,23 +83,81 @@
                 out_ref[(order * 2 + part) * (degree_dev // 128) + cut] = block.astype(jnp.bfloat16)
 
 
-def level_sums(poloidal, toroidal):
+def halves(x):
+    high = x.astype(jnp.bfloat16)
+    return high, (x - high.astype(jnp.float32)).astype(jnp.bfloat16)
+
+
+def weight_rows(orders_ref, weight_ref):
+    order = orders_ref[own_order()]
+    cut = lax.broadcasted_iota(jnp.int32, weight_ref.shape, 0)
+    lane = lax.broadcasted_iota(jnp.int32, weight_ref.shape, 1)
+    degree = (lax.axis_index(TAB) * weight_ref.shape[0] + cut) * weight_ref.shape[1] + lane
+    degree_wide = degree.astype(jnp.float32)
+    weight = jnp.sqrt(degree_wide * (degree_wide + 1.0))
+    weight_ref[...] = jnp.where(degree >= order, weight, 0.0)
+
+
+def longitude_rows(orders_ref, phase_ref):
+    order_count = orders_ref.shape[0]
+    points = phase_ref.shape[1]
+    row = lax.broadcasted_iota(jnp.int32, (order_count, 128), 0)
+    lane = lax.broadcasted_iota(jnp.int32, (order_count, 128), 1).astype(jnp.float32)
+    order = jnp.zeros((order_count, 128), jnp.int32)
+    for at in range(order_count):
+        order = jnp.where(row == at, orders_ref[at], order)
+    order = order.astype(jnp.float32)
+    first = order * lane
+    quarter = points // 4
+    for start in range(0, points, 128):
+        turn = first + order * float(start)
+        quarters = jnp.floor(turn * (1.0 / quarter) + 0.5)
+        x = (turn - quarters * float(quarter)) * (2.0 * math.pi / points)
+        z = x * x
+        sine = x * (1 + z * (-1 / 6 + z * (1 / 120 + z * (-1 / 5040 + z * (1 / 362880)))))
+        cosine = 1 + z * (-1 / 2 + z * (1 / 24 + z * (-1 / 720 + z * (1 / 40320))))
+        quarters = quarters.astype(jnp.int32)
+        odd = (quarters & 1) == 1
+        cos_row = jnp.where(odd, sine, cosine)
+        sin_row = jnp.where(odd, cosine, sine)
+        cos_row = jnp.where(((quarters + 1) & 2) == 0, 2.0, -2.0) * cos_row
+        sin_row = jnp.where((quarters & 2) == 0, -2.0, 2.0) * sin_row
+        cos_high, cos_low = halves(cos_row)
+        sin_high, sin_low = halves(sin_row)
+        for at, rows in enumerate([cos_high, sin_high, cos_low, sin_low, cos_high, sin_high]):
+            phase_ref[at * order_count : (at + 1) * order_count, start : start + 128] = rows
+
+
+def near_place():
+    return (1 - lax.axis_index("xl")) * 4 + lax.rem(lax.axis_index("zn") + 3, 4)
+
+
+def own_order():
+    return lax.axis_index("c") * len(NEAR_ORDER) + near_place()
+
+
+def level_sums(poloidal, toroidal, orders):
     level_dev, order_count, _, degree_dev = poloidal.shape
+    constants = level_constants(level_dev)
     return pl.pallas_call(
         level_kernel,
-        out_shape=jax.ShapeDtypeStruct(
-            (order_count * 2 * degree_dev // 128, 3 * SHELLS, 128), jnp.bfloat16
+        out_shape=(
+            pltpu.VMEM((order_count * 2 * degree_dev // 128, 3 * SHELLS, 128), jnp.bfloat16),
+            pltpu.VMEM((6 * order_count, NPHI), jnp.bfloat16),
+            pltpu.VMEM((degree_dev // 128, 128), jnp.float32),
         ),
-        compiler_params=pltpu.CompilerParams(vmem_limit_bytes=60 << 20),
+        in_specs=[pl.BlockSpec(memory_space=pltpu.HBM)] * 4,
+        out_specs=[pl.BlockSpec(memory_space=pltpu.VMEM)] * 3,
+        scratch_shapes=[
+            pltpu.VMEM(constants.shape, jnp.float32),
+            pltpu.VMEM(poloidal.shape, jnp.bfloat16),
+            pltpu.VMEM(toroidal.shape, jnp.bfloat16),
+            pltpu.SMEM(orders.shape, jnp.int32),
+            pltpu.SemaphoreType.DMA((4,)),
+        ],
+        compiler_params=pltpu.CompilerParams(vmem_limit_bytes=57_000_000),
         name="level_sums",
-    )(level_constants(level_dev), poloidal, toroidal)
-
-
-def longitude_table(orders, points):
-    positions = jnp.arange(points, dtype=jnp.int32)
-    turn_counts = orders[:, None] * positions[None, :] % points
-    angles = 2.0 * math.pi / points * turn_counts.astype(jnp.float32)
-    return jnp.concatenate([2.0 * jnp.cos(angles), -2.0 * jnp.sin(angles)], axis=0)
+    )(constants, poloidal, toroidal, orders)
 
 
 def split_bf16(x):
@@ -91,42 +170,26 @@
 
 
 def on_device(poloidal, toroidal, tables, orders):
-    c = lax.axis_index("c")
-    tab = lax.axis_index(TAB)
     _, order_count, _, degree_dev = poloidal.shape
     half = order_count // 2
     blocks = half * 2 * degree_dev // 128
-    near = (1 - lax.axis_index("xl")) * 4 + (lax.axis_index("zn") + 3) % 4
     near_count = lax.axis_size(NEAR)
     far_count = lax.axis_size("zf")
-    own_order = c * half + near
-    first_degree = tab * degree_dev
-    first_block = c * blocks
-    partial = level_sums(poloidal, toroidal)
-    partial, own_order, first_degree, first_block = lax.optimization_barrier(
-        (partial, own_order, first_degree, first_block)
-    )
+    first_block = lax.axis_index("c") * blocks
+    partial, phases, weight = level_sums(poloidal, toroidal, orders)
     pair = lax.all_gather(partial, "c", axis=0)
     pair = lax.dynamic_slice_in_dim(pair, first_block, blocks, 1).astype(jnp.float32)
     partial = (pair[0] + pair[1]).astype(jnp.bfloat16)
     shares = lax.all_to_all(partial, NEAR, 0, 0, axis_index_groups=[NEAR_ORDER], tiled=True)
     shares = shares.reshape(near_count, -1, 3 * SHELLS, 128).astype(jnp.float32)
-    near_sum = lax.optimization_barrier(jnp.sum(shares, axis=0))
+    near_sum, tables = lax.optimization_barrier((jnp.sum(shares, axis=0), tables))
     copies = jnp.broadcast_to(near_sum.astype(jnp.bfloat16), (far_count,) + near_sum.shape)
-    copies, orders, tables = lax.optimization_barrier((copies, orders, tables))
+    pair_table = jnp.concatenate([tables[1], tables[2]], axis=-1)
+    copies, plain_table, pair_table = lax.optimization_barrier((copies, tables[0], pair_table))
     shares = lax.all_to_all(copies, "zf", 0, 0, axis_index_groups=[FAR_ORDER], tiled=True)
-    order = jnp.sum(jnp.where(jnp.arange(order_count) == own_order, orders, 0))
-    degree = first_degree + jnp.arange(degree_dev, dtype=jnp.int32)
-    degree_wide = degree.astype(jnp.float32)
-    weight = jnp.where(degree >= order, jnp.sqrt(degree_wide * (degree_wide + 1.0)), 0.0)
-    weight = weight.reshape(1, degree_dev // 128, 1, 128)
-    p_hi, p_lo = split_bf16(longitude_table(orders, NPHI))
-    pair_table = jnp.concatenate([tables[1], tables[2]], axis=-1)
-    shares, weight, p_hi, p_lo, plain_table, pair_table = lax.optimization_barrier(
-        (shares, weight, p_hi, p_lo, tables[0], pair_table)
-    )
     radial = jnp.sum(shares.astype(jnp.float32), axis=0)
     radial = radial.reshape(2, degree_dev // 128, 3, SHELLS, 128)
+    weight = weight.reshape(1, degree_dev // 128, 1, 128)
     spheroidal = radial[:, :, 0] / shell_radius()[:, None]
     spectra = jnp.stack(
         [
@@ -160,7 +223,7 @@
     f_hi, f_lo = split_bf16(summed)
     values = lax.dot_general(
         jnp.concatenate([f_hi, f_hi, f_lo]),
-        jnp.concatenate([p_hi, p_lo, p_hi]),
+        phases,
         (((0,), (0,)), ((), ())),
         preferred_element_type=jnp.float32,
     )

time: 64.9 us -> 63.6 us (0.980)
  blocking collectives: 43.2 us -> 58.1 us
  starting transfers between devices: 12 us -> 0 us
  other arithmetic: 3.51 us -> 0.44 us
  local copies, waits for them, and re-layouts: 1.17 us -> 0.51 us
    all_to_all x0 -> x1, blocking collectives: none -> 15 us  [on_device(): lax.all_to_all(copies, 'zf', 0, 0, axis_index_groups=[FAR_ORDER], tiled=T...]
    all_to_all x1 -> x0, starting transfers between devices: 12 us -> none  [on_device(): lax.all_to_all(copies, 'zf', 0, 0, axis_index_groups=[FAR_ORDER], tiled=T...]
    mul x1 -> x0, other arithmetic: 1.68 us -> none  [longitude_table(): 2.0 * jnp.cos(angles)]
    reduce_sum x2 -> x1, other arithmetic: 0.69 us -> 0.03 us  [on_device(): jnp.sum(shares, axis=0)]
  transfers between devices with their start and end apart: 1 -> 0, of which waited for: 0 -> 0; matrix products, arithmetic and copies ran while one was open for 5% -> 0% of each run, Pallas kernels for 0% -> 0%
where the time goes in v6:
time: 63.6 us; the launch traced here: 63.3 us
  blocking collectives  58.1 us (91%)
  matrix products  2.38 us (4%)
  Pallas kernels  1.7 us (3%)
    all_to_all x1, blocking collectives, on_device(): lax.all_to_all(copies, 'zf', 0, 0, axis_index_groups=[FAR_ORDER], tiled=T...  15 us
    all_to_all x1, blocking collectives, on_device(): lax.all_to_all(fourier.astype(jnp.bfloat16), TAB, 0, 0, axis_index_groups...  10.9 us
    all_to_all x1, blocking collectives, on_device(): lax.all_to_all(partial, NEAR, 0, 0, axis_index_groups=[NEAR_ORDER], tiled...  9.13 us
    all_gather x1, blocking collectives, on_device(): pair = lax.all_gather(partial, 'c', axis=0)  8.87 us
    all_to_all x1, blocking collectives, on_device(): lax.all_to_all(spectra, NEAR, 0, 0, axis_index_groups=[NEAR_ORDER], tiled...  8.25 us
    all_gather x1, blocking collectives, on_device(): spectra = lax.all_gather(spectra, 'c', axis=0, tiled=True)  5.92 us
    dot_general x1, matrix products, on_device(): lax.dot_general(jnp.concatenate([f_hi, f_hi, f_lo]), phases, (((0,), (0,)...  1.86 us
    pallas_call x1, Pallas kernels, level_sums(): pl.pallas_call(level_kernel, out_shape=(pltpu.VMEM((order_count * 2 * deg...  1.7 us

profile of v6, /device:TPU:1, one launch (start us, length us, event | category | flops | bytes accessed | tf_op | source)
XLA Modules:
  0.0 63.3 jit_solution(9805531370559481908)
XLA Ops:
  0.0 1.7 %level_sums.1 = (bf16[64,24,128]{2,1,0:T(8,128)(2,1)S(1)}, bf16[96,6144]{1,0:T(8,128)(2,1)S(1)}, f32[2,128]{1,0:T(2,128)S(1)}) custom-call(f32[2,2,48,128]{3,2,1,0:T(8,128)} %constant.16.clone.constant_hbm, bf16[16,16,2,256]{3,2,1,0:T(2,128)(2,1)} %pol_hbm.1, bf16[16,16,2,256]{3,2,1,0:T(2,128)(2,1)} %tor_hbm.1, s32[16]{0:T(128)} %orders_hbm.1), custom_call_target="tpu_custom_call" | custom-call | tf_op jit(solution)/shard_map/level_sums/pallas_call | solution.py:142
  1.7 8.9 %all-gather = bf16[128,24,128]{2,1,0:T(8,128)(2,1)S(1)} all-gather(bf16[64,24,128]{2,1,0:T(8,128)(2,1)S(1)} %get-tuple-element.13), channel_id=2, replica_groups=mesh['xh'=2,'y'=4,'xl'=2,'zf'=4,'zn'=4,'c'=2] {'c'}, dimensions={0}, use_global_device_ids=true | all-gather | bytes 1179648 | tf_op jit(solution)/shard_map/all_gather | solution.py:180
  10.6 0.0 copy-start
  10.6 0.1 dynamic-slice_convert_fusion
  10.7 9.1 %all_to_all.20 = bf16[32,24,128]{2,1,0:T(8,128)(2,1)S(1)} all-to-all(bf16[32,24,128]{2,1,0:T(8,128)(2,1)S(1)} %fusion.16), channel_id=1, replica_groups={{34,36,38,32,2,4,6,0},{35,37,39,33,3,5,7,1},{42,44,46,40,10,12,14,8},{4..., dimensions={0} | all-to-all | bytes 393216 | tf_op jit(solution)/shard_map/all_to_all | solution.py:183
  19.8 0.0 copy-done
  19.9 0.1 slice_bitcast_fusion.1
  19.9 0.0 copy-start.1
  20.0 0.1 pad_maximum_fusion
  20.1 15.0 %all_to_all.21 = bf16[4,4,24,128]{3,2,1,0:T(8,128)(2,1)S(1)} all-to-all(bf16[4,4,24,128]{3,2,1,0:T(8,128)(2,1)S(1)} %broadcast_in_dim.4), channel_id=1, replica_groups={{16,24,0,8},{17,25,1,9},{18,26,2,10},{19,27,3,11},{20,28,4,12},{21,29,5..., dimensions={0} | all-to-all | bytes 196608 | tf_op jit(solution)/shard_map/all_to_all | solution.py:189
  35.1 0.0 copy-done.1
  35.1 0.1 multiply_convert_fusion
  35.3 8.3 %all_to_all.22 = bf16[8,4,24,128]{3,2,1,0:T(8,128)(2,1)S(1)} all-to-all(bf16[8,4,24,128]{3,2,1,0:T(8,128)(2,1)S(1)} %broadcast_in_dim.10), channel_id=1, replica_groups={{34,36,38,32,2,4,6,0},{35,37,39,33,3,5,7,1},{42,44,46,40,10,12,14,8},{4..., dimensions={0} | all-to-all | bytes 393216 | tf_op jit(solution)/shard_map/all_to_all | solution.py:205
  43.5 5.9 %all_gather.11 = bf16[16,4,24,128]{3,2,1,0:T(8,128)(2,1)S(1)} all-gather(bf16[8,4,24,128]{3,2,1,0:T(8,128)(2,1)S(1)} %all_to_all.22), channel_id=1, replica_groups=mesh['xh'=2,'y'=4,'xl'=2,'zf'=4,'zn'=4,'c'=2] {'c'}, dimensions={0}, use_global_device_ids=true | all-gather | bytes 589824 | tf_op jit(solution)/shard_map/all_gather | solution.py:206
  49.5 0.2 fusion.1
  49.7 0.3 fusion
  50.1 0.1 maximum_bitcast_fusion
  50.1 0.2 copy.12
  50.3 0.2 convert_element_type.57
  50.5 10.9 %all_to_all.23 = bf16[8,32,144]{2,1,0:T(8,128)(2,1)S(1)} all-to-all(bf16[8,32,144]{2,1,0:T(8,128)(2,1)S(1)} %convert_element_type.57), channel_id=1, replica_groups={{448,384,320,256,192,128,64,0},{449,385,321,257,193,129,65,1},{450,386,..., dimensions={0} | all-to-all | bytes 147456 | tf_op jit(solution)/shard_map/all_to_all | solution.py:219
  61.4 1.9 %convolution_convert_fusion = bf16[144,6144]{1,0:T(8,128)(2,1)} fusion(bf16[96,6144]{1,0:T(8,128)(2,1)S(1)} %get-tuple-element.20, bf16[32,144]{1,0:T(8,128)(2,1)S(1)} %get-tuple-element.36, bf16[32,144]{1,0:T(8,128)(2,1)S(1)} %get-tuple-element.35), kind=kOutput, calls=%fused_computation | convolution fusion | flops 170836992 | bytes 2967552 | tf_op jit(solution)/shard_map/dot_general | solution.py:224
  (12 shorter events, 0.3 us)
Async XLA Ops:
  10.6 9.3 %copy-start = (bf16[3,16,48,256]{3,2,1,0:T(8,128)(2,1)S(1)}, bf16[3,16,48,256]{3,2,1,0:T(8,128)(2,1)}, u32[]{:S(2)}) copy-start(bf16[3,16,48,256]{3,2,1,0:T(8,128)(2,1)} %param.8) | copy-start | bytes 3538948
  19.9 15.2 %copy-start.1 = (f32[8]{0:T(128)S(1)}, f32[8]{0:T(128)}, u32[]{:S(2)}) copy-start(f32[8]{0:T(128)} %constant.22) | copy-start | bytes 100

commit v7 on v6

--- a/solution.py
+++ b/solution.py
@@ -14,7 +14,7 @@
 NEAR = ("xl", "zn")
 NEAR_ORDER = (5, 6, 7, 4, 1, 2, 3, 0)
 FAR_ORDER = (2, 3, 0, 1)
-TAB_ORDER = (7, 6, 5, 4, 3, 2, 1, 0)
+TAB_ORDER = (6, 2, 7, 3, 5, 1, 4, 0)
 TAB = ("xh", "y")
 
 
@@ -160,13 +160,46 @@
     )(constants, poloidal, toroidal, orders)
 
 
-def split_bf16(x):
-    hi = lax.reduce_precision(x, 8, 7)
-    return hi.astype(jnp.bfloat16), (x - hi).astype(jnp.bfloat16)
-
-
 def dot32(a, b):
     return jnp.dot(a, b, preferred_element_type=jnp.float32)
+
+
+def synthesis_kernel(share_ref, phase_ref, out_hbm, chunk_ref, sems):
+    chunks, _, width = chunk_ref.shape
+    high, low = halves(jnp.sum(share_ref[...].astype(jnp.float32), axis=0))
+    rows = jnp.concatenate([high, high, low], axis=0)
+    copies = []
+    for at in range(chunks):
+        columns = slice(at * width, (at + 1) * width)
+        values = lax.dot_general(
+            rows,
+            phase_ref[:, columns],
+            (((0,), (0,)), ((), ())),
+            preferred_element_type=jnp.float32,
+        )
+        chunk_ref[at] = values.astype(jnp.bfloat16)
+        copies.append(
+            pltpu.make_async_copy(chunk_ref.at[at], out_hbm.at[:, columns], sems.at[at])
+        )
+        copies[-1].start()
+    for copy in copies:
+        copy.wait()
+
+
+def synthesis(shares, phases, chunks):
+    rows, points = shares.shape[2], phases.shape[1]
+    return pl.pallas_call(
+        synthesis_kernel,
+        out_shape=jax.ShapeDtypeStruct((rows, points), jnp.bfloat16),
+        in_specs=[pl.BlockSpec(memory_space=pltpu.VMEM)] * 2,
+        out_specs=pl.BlockSpec(memory_space=pltpu.HBM),
+        scratch_shapes=[
+            pltpu.VMEM((chunks, rows, points // chunks), jnp.bfloat16),
+            pltpu.SemaphoreType.DMA((chunks,)),
+        ],
+        compiler_params=pltpu.CompilerParams(vmem_limit_bytes=16 << 20),
+        name="synthesis",
+    )(shares, phases)
 
 
 def on_device(poloidal, toroidal, tables, orders):
@@ -219,15 +252,7 @@
     fourier = lax.all_to_all(
         fourier.astype(jnp.bfloat16), TAB, 0, 0, axis_index_groups=[TAB_ORDER], tiled=True
     )
-    summed = jnp.sum(fourier.astype(jnp.float32), axis=0)
-    f_hi, f_lo = split_bf16(summed)
-    values = lax.dot_general(
-        jnp.concatenate([f_hi, f_hi, f_lo]),
-        phases,
-        (((0,), (0,)), ((), ())),
-        preferred_element_type=jnp.float32,
-    )
-    return values.astype(jnp.bfloat16).reshape(3, 1, -1, NPHI)
+    return synthesis(fourier, phases, 4).reshape(3, 1, -1, NPHI)
 
 
 def solution(mesh):

time: 63.6 us -> 62.5 us (0.983)
  matrix products: 2.38 us -> 0.53 us
  Pallas kernels: 1.7 us -> 3.24 us
  blocking collectives: 58.1 us -> 57.4 us
    dot_general x1 -> x0, matrix products: 1.86 us -> none  [on_device(): lax.dot_general(jnp.concatenate([f_hi, f_hi, f_lo]), phases, (((0,), (0,)...]
    pallas_call x0 -> x1, Pallas kernels: none -> 1.54 us  [synthesis(): pl.pallas_call(synthesis_kernel, out_shape=jax.ShapeDtypeStruct((rows, po...]
    all_to_all x1, blocking collectives: 10.9 us -> 10.2 us  [on_device(): lax.all_to_all(fourier.astype(jnp.bfloat16), TAB, 0, 0, axis_index_groups...]
where the time goes in v7:
time: 62.5 us; the launch traced here: 62.2 us
  blocking collectives  57.4 us (92%)
  Pallas kernels  3.24 us (5%)
    all_to_all x1, blocking collectives, on_device(): lax.all_to_all(copies, 'zf', 0, 0, axis_index_groups=[FAR_ORDER], tiled=T...  15 us
    all_to_all x1, blocking collectives, on_device(): lax.all_to_all(fourier.astype(jnp.bfloat16), TAB, 0, 0, axis_index_groups...  10.2 us
    all_to_all x1, blocking collectives, on_device(): lax.all_to_all(partial, NEAR, 0, 0, axis_index_groups=[NEAR_ORDER], tiled...  9.13 us
    all_gather x1, blocking collectives, on_device(): pair = lax.all_gather(partial, 'c', axis=0)  8.87 us
    all_to_all x1, blocking collectives, on_device(): lax.all_to_all(spectra, NEAR, 0, 0, axis_index_groups=[NEAR_ORDER], tiled...  8.25 us
    all_gather x1, blocking collectives, on_device(): spectra = lax.all_gather(spectra, 'c', axis=0, tiled=True)  5.92 us
    pallas_call x1, Pallas kernels, level_sums(): pl.pallas_call(level_kernel, out_shape=(pltpu.VMEM((order_count * 2 * deg...  1.7 us
    pallas_call x1, Pallas kernels, synthesis(): pl.pallas_call(synthesis_kernel, out_shape=jax.ShapeDtypeStruct((rows, po...  1.54 us

profile of v7, /device:TPU:1, one launch (start us, length us, event | category | flops | bytes accessed | tf_op | source)
XLA Modules:
  0.0 62.2 jit_solution(9358286075355100020)
XLA Ops:
  0.0 1.7 %level_sums.1 = (bf16[64,24,128]{2,1,0:T(8,128)(2,1)S(1)}, bf16[96,6144]{1,0:T(8,128)(2,1)S(1)}, f32[2,128]{1,0:T(2,128)S(1)}) custom-call(f32[2,2,48,128]{3,2,1,0:T(8,128)} %constant.16.clone.constant_hbm, bf16[16,16,2,256]{3,2,1,0:T(2,128)(2,1)} %pol_hbm.1, bf16[16,16,2,256]{3,2,1,0:T(2,128)(2,1)} %tor_hbm.1, s32[16]{0:T(128)} %orders_hbm.1), custom_call_target="tpu_custom_call" | custom-call | tf_op jit(solution)/shard_map/level_sums/pallas_call | solution.py:142
  1.7 8.9 %all-gather = bf16[128,24,128]{2,1,0:T(8,128)(2,1)S(1)} all-gather(bf16[64,24,128]{2,1,0:T(8,128)(2,1)S(1)} %get-tuple-element.13), channel_id=2, replica_groups=mesh['xh'=2,'y'=4,'xl'=2,'zf'=4,'zn'=4,'c'=2] {'c'}, dimensions={0}, use_global_device_ids=true | all-gather | bytes 1179648 | tf_op jit(solution)/shard_map/all_gather | solution.py:213
  10.6 0.0 copy-start
  10.6 0.1 dynamic-slice_convert_fusion
  10.7 9.1 %all_to_all.20 = bf16[32,24,128]{2,1,0:T(8,128)(2,1)S(1)} all-to-all(bf16[32,24,128]{2,1,0:T(8,128)(2,1)S(1)} %fusion.16), channel_id=1, replica_groups={{34,36,38,32,2,4,6,0},{35,37,39,33,3,5,7,1},{42,44,46,40,10,12,14,8},{4..., dimensions={0} | all-to-all | bytes 393216 | tf_op jit(solution)/shard_map/all_to_all | solution.py:216
  19.8 0.0 copy-done
  19.9 0.1 slice_bitcast_fusion.1
  19.9 0.0 copy-start.1
  20.0 0.1 pad_maximum_fusion
  20.1 15.0 %all_to_all.21 = bf16[4,4,24,128]{3,2,1,0:T(8,128)(2,1)S(1)} all-to-all(bf16[4,4,24,128]{3,2,1,0:T(8,128)(2,1)S(1)} %broadcast_in_dim.4), channel_id=1, replica_groups={{16,24,0,8},{17,25,1,9},{18,26,2,10},{19,27,3,11},{20,28,4,12},{21,29,5..., dimensions={0} | all-to-all | bytes 196608 | tf_op jit(solution)/shard_map/all_to_all | solution.py:222
  35.1 0.0 copy-done.1
  35.1 0.1 multiply_convert_fusion
  35.3 8.3 %all_to_all.22 = bf16[8,4,24,128]{3,2,1,0:T(8,128)(2,1)S(1)} all-to-all(bf16[8,4,24,128]{3,2,1,0:T(8,128)(2,1)S(1)} %broadcast_in_dim.10), channel_id=1, replica_groups={{34,36,38,32,2,4,6,0},{35,37,39,33,3,5,7,1},{42,44,46,40,10,12,14,8},{4..., dimensions={0} | all-to-all | bytes 393216 | tf_op jit(solution)/shard_map/all_to_all | solution.py:238
  43.5 5.9 %all_gather.11 = bf16[16,4,24,128]{3,2,1,0:T(8,128)(2,1)S(1)} all-gather(bf16[8,4,24,128]{3,2,1,0:T(8,128)(2,1)S(1)} %all_to_all.22), channel_id=1, replica_groups=mesh['xh'=2,'y'=4,'xl'=2,'zf'=4,'zn'=4,'c'=2] {'c'}, dimensions={0}, use_global_device_ids=true | all-gather | bytes 589824 | tf_op jit(solution)/shard_map/all_gather | solution.py:239
  49.5 0.2 fusion.1
  49.7 0.3 fusion
  50.1 0.1 maximum_bitcast_fusion
  50.1 0.2 copy.13
  50.3 0.2 convert_element_type.45
  50.5 10.2 %all_to_all.23.share_ref = bf16[8,32,144]{2,1,0:T(8,128)(2,1)S(1)} all-to-all(bf16[8,32,144]{2,1,0:T(8,128)(2,1)S(1)} %convert_element_type.45), channel_id=1, replica_groups={{384,128,448,192,320,64,256,0},{385,129,449,193,321,65,257,1},{386,130,..., dimensions={0} | all-to-all | bytes 147456 | tf_op jit(solution)/shard_map/all_to_all | solution.py:252
  60.7 1.5 %synthesis.1 = bf16[144,6144]{1,0:T(8,128)(2,1)} custom-call(bf16[8,32,144]{2,1,0:T(8,128)(2,1)S(1)} %all_to_all.23.share_ref, bf16[96,6144]{1,0:T(8,128)(2,1)S(1)} %get-tuple-element.20.phase_ref), custom_call_target="tpu_custom_call" | custom-call | tf_op jit(solution)/shard_map/synthesis/pallas_call | solution.py:191
  (10 shorter events, 0.2 us)
Async XLA Ops:
  10.6 9.3 %copy-start = (bf16[3,16,48,256]{3,2,1,0:T(8,128)(2,1)S(1)}, bf16[3,16,48,256]{3,2,1,0:T(8,128)(2,1)}, u32[]{:S(2)}) copy-start(bf16[3,16,48,256]{3,2,1,0:T(8,128)(2,1)} %param.8) | copy-start | bytes 3538948
  19.9 15.2 %copy-start.1 = (f32[8]{0:T(128)S(1)}, f32[8]{0:T(128)}, u32[]{:S(2)}) copy-start(f32[8]{0:T(128)} %constant.22) | copy-start | bytes 100

commit v8 on v7

--- a/solution.py
+++ b/solution.py
@@ -164,6 +164,59 @@
     return jnp.dot(a, b, preferred_element_type=jnp.float32)
 
 
+def projection_kernel(spectra_ref, table_ref, out_ref, held_ref):
+    order_count = table_ref.shape[1]
+    cuts = spectra_ref.shape[1] // 2
+
+    def project(rows, table):
+        return lax.dot_general(
+            jnp.concatenate(rows, axis=0).astype(jnp.bfloat16),
+            table,
+            (((1,), (1,)), ((), ())),
+            preferred_element_type=jnp.float32,
+        )
+
+    for order in range(order_count):
+        blocks = [spectra_ref[order, at].astype(jnp.float32) for at in range(2 * cuts)]
+        (q_re, q_im), (s_re, s_im), (t_re, t_im) = (
+            [
+                jnp.concatenate(
+                    [
+                        block[kind * SHELLS : (kind + 1) * SHELLS]
+                        for block in blocks[part * cuts : (part + 1) * cuts]
+                    ],
+                    axis=1,
+                )
+                for part in range(2)
+            ]
+            for kind in range(3)
+        )
+        held_ref[0, order] = project([q_re, q_im], table_ref[0, order])
+        pair = project([s_re, s_im, -t_re, -t_im], table_ref[1, order])
+        pair += project([-t_im, t_re, -s_im, s_re], table_ref[2, order])
+        held_ref[1, order] = pair[: 2 * SHELLS]
+        held_ref[2, order] = pair[2 * SHELLS :]
+    for shell in range(SHELLS):
+        for part in range(2):
+            rows = [held_ref[kind, :, part * SHELLS + shell, :] for kind in range(3)]
+            out_ref[shell, part * order_count : (part + 1) * order_count, :] = jnp.concatenate(
+                rows, axis=1
+            ).astype(jnp.bfloat16)
+
+
+def projection(spectra, tables):
+    kinds, order_count, latitudes, _ = tables.shape
+    return pl.pallas_call(
+        projection_kernel,
+        out_shape=pltpu.VMEM((SHELLS, 2 * order_count, kinds * latitudes), jnp.bfloat16),
+        in_specs=[pl.BlockSpec(memory_space=pltpu.VMEM)] * 2,
+        out_specs=pl.BlockSpec(memory_space=pltpu.VMEM),
+        scratch_shapes=[pltpu.VMEM((kinds, order_count, 2 * SHELLS, latitudes), jnp.float32)],
+        compiler_params=pltpu.CompilerParams(vmem_limit_bytes=16 << 20),
+        name="projection",
+    )(spectra, tables)
+
+
 def synthesis_kernel(share_ref, phase_ref, out_hbm, chunk_ref, sems):
     chunks, _, width = chunk_ref.shape
     high, low = halves(jnp.sum(share_ref[...].astype(jnp.float32), axis=0))
@@ -215,10 +268,8 @@
     partial = (pair[0] + pair[1]).astype(jnp.bfloat16)
     shares = lax.all_to_all(partial, NEAR, 0, 0, axis_index_groups=[NEAR_ORDER], tiled=True)
     shares = shares.reshape(near_count, -1, 3 * SHELLS, 128).astype(jnp.float32)
-    near_sum, tables = lax.optimization_barrier((jnp.sum(shares, axis=0), tables))
+    near_sum = lax.optimization_barrier(jnp.sum(shares, axis=0))
     copies = jnp.broadcast_to(near_sum.astype(jnp.bfloat16), (far_count,) + near_sum.shape)
-    pair_table = jnp.concatenate([tables[1], tables[2]], axis=-1)
-    copies, plain_table, pair_table = lax.optimization_barrier((copies, tables[0], pair_table))
     shares = lax.all_to_all(copies, "zf", 0, 0, axis_index_groups=[FAR_ORDER], tiled=True)
     radial = jnp.sum(shares.astype(jnp.float32), axis=0)
     radial = radial.reshape(2, degree_dev // 128, 3, SHELLS, 128)
@@ -237,21 +288,8 @@
     )
     spectra = lax.all_to_all(spectra, NEAR, 0, 0, axis_index_groups=[NEAR_ORDER], tiled=True)
     spectra = lax.all_gather(spectra, "c", axis=0, tiled=True)
-    coef = spectra.reshape(order_count, 2, 2, 3, SHELLS, 128).transpose(3, 0, 4, 1, 2, 5)
-    coef = coef.reshape(3, order_count, SHELLS, 2, degree_dev)
-
-    q, s, t = coef[0], coef[1], coef[2]
-    swap = lambda v: jnp.stack([-v[:, :, 1], v[:, :, 0]], axis=2)
-    theta = jnp.concatenate([s, swap(t)], axis=-1)
-    phi = jnp.concatenate([-t, swap(s)], axis=-1)
-    both = jnp.concatenate([theta, phi], axis=1)
-    plain = jnp.einsum("mscl,mal->mcsa", q, plain_table, preferred_element_type=jnp.float32)
-    pair = jnp.einsum("mscl,mal->mcsa", both, pair_table, preferred_element_type=jnp.float32)
-    fourier = jnp.stack([plain, pair[:, :, :SHELLS], pair[:, :, SHELLS:]])
-    fourier = fourier.transpose(3, 2, 1, 0, 4).reshape(SHELLS, 2 * order_count, -1)
-    fourier = lax.all_to_all(
-        fourier.astype(jnp.bfloat16), TAB, 0, 0, axis_index_groups=[TAB_ORDER], tiled=True
-    )
+    fourier = projection(spectra.reshape(order_count, -1, 3 * SHELLS, 128), tables)
+    fourier = lax.all_to_all(fourier, TAB, 0, 0, axis_index_groups=[TAB_ORDER], tiled=True)
     return synthesis(fourier, phases, 4).reshape(3, 1, -1, NPHI)
 
 

time: 62.5 us -> 61.9 us (level)
  no operation moved by 1% of the time
where the time goes in v8:
time: 61.9 us; the launch traced here: 61.6 us
  blocking collectives  57.4 us (93%)
  Pallas kernels  3.83 us (6%)
    all_to_all x1, blocking collectives, on_device(): lax.all_to_all(copies, 'zf', 0, 0, axis_index_groups=[FAR_ORDER], tiled=T...  15 us
    all_to_all x1, blocking collectives, on_device(): lax.all_to_all(fourier, TAB, 0, 0, axis_index_groups=[TAB_ORDER], tiled=T...  10.2 us
    all_to_all x1, blocking collectives, on_device(): lax.all_to_all(partial, NEAR, 0, 0, axis_index_groups=[NEAR_ORDER], tiled...  9.13 us
    all_gather x1, blocking collectives, on_device(): pair = lax.all_gather(partial, 'c', axis=0)  8.87 us
    all_to_all x1, blocking collectives, on_device(): lax.all_to_all(spectra, NEAR, 0, 0, axis_index_groups=[NEAR_ORDER], tiled...  8.25 us
    all_gather x1, blocking collectives, on_device(): spectra = lax.all_gather(spectra, 'c', axis=0, tiled=True)  5.92 us
    pallas_call x1, Pallas kernels, level_sums(): pl.pallas_call(level_kernel, out_shape=(pltpu.VMEM((order_count * 2 * deg...  1.7 us
    pallas_call x1, Pallas kernels, synthesis(): pl.pallas_call(synthesis_kernel, out_shape=jax.ShapeDtypeStruct((rows, po...  1.54 us

profile of v8, /device:TPU:1, one launch (start us, length us, event | category | flops | bytes accessed | tf_op | source)
XLA Modules:
  0.0 61.6 jit_solution(4864371561395087232)
XLA Ops:
  0.0 1.7 %level_sums.1 = (bf16[64,24,128]{2,1,0:T(8,128)(2,1)S(1)}, bf16[96,6144]{1,0:T(8,128)(2,1)S(1)}, f32[2,128]{1,0:T(2,128)S(1)}) custom-call(f32[2,2,48,128]{3,2,1,0:T(8,128)} %constant.16.clone.constant_hbm, bf16[16,16,2,256]{3,2,1,0:T(2,128)(2,1)} %pol_hbm.1, bf16[16,16,2,256]{3,2,1,0:T(2,128)(2,1)} %tor_hbm.1, s32[16]{0:T(128)} %orders_hbm.1), custom_call_target="tpu_custom_call" | custom-call | tf_op jit(solution)/shard_map/level_sums/pallas_call | solution.py:142
  1.7 8.9 %all-gather = bf16[128,24,128]{2,1,0:T(8,128)(2,1)S(1)} all-gather(bf16[64,24,128]{2,1,0:T(8,128)(2,1)S(1)} %get-tuple-element.9), channel_id=2, replica_groups=mesh['xh'=2,'y'=4,'xl'=2,'zf'=4,'zn'=4,'c'=2] {'c'}, dimensions={0}, use_global_device_ids=true | all-gather | bytes 1179648 | tf_op jit(solution)/shard_map/all_gather | solution.py:266
  10.6 0.1 dynamic-slice_convert_fusion
  10.6 0.0 copy-start.1
  10.7 0.0 copy-start
  10.7 9.1 %all_to_all.20 = bf16[32,24,128]{2,1,0:T(8,128)(2,1)S(1)} all-to-all(bf16[32,24,128]{2,1,0:T(8,128)(2,1)S(1)} %fusion.1), channel_id=1, replica_groups={{34,36,38,32,2,4,6,0},{35,37,39,33,3,5,7,1},{42,44,46,40,10,12,14,8},{4..., dimensions={0} | all-to-all | bytes 393216 | tf_op jit(solution)/shard_map/all_to_all | solution.py:269
  19.9 15.0 %all_to_all.21 = bf16[4,4,24,128]{3,2,1,0:T(8,128)(2,1)S(1)} all-to-all(bf16[4,4,24,128]{3,2,1,0:T(8,128)(2,1)S(1)} %broadcast_in_dim.4), channel_id=1, replica_groups={{16,24,0,8},{17,25,1,9},{18,26,2,10},{19,27,3,11},{20,28,4,12},{21,29,5..., dimensions={0} | all-to-all | bytes 196608 | tf_op jit(solution)/shard_map/all_to_all | solution.py:273
  35.0 0.0 copy-done.1
  35.0 0.1 multiply_convert_fusion
  35.1 8.3 %all_to_all.22 = bf16[8,4,24,128]{3,2,1,0:T(8,128)(2,1)S(1)} all-to-all(bf16[8,4,24,128]{3,2,1,0:T(8,128)(2,1)S(1)} %broadcast_in_dim.10), channel_id=1, replica_groups={{34,36,38,32,2,4,6,0},{35,37,39,33,3,5,7,1},{42,44,46,40,10,12,14,8},{4..., dimensions={0} | all-to-all | bytes 393216 | tf_op jit(solution)/shard_map/all_to_all | solution.py:289
  43.3 5.9 %all_gather.11.spectra_ref = bf16[16,4,24,128]{3,2,1,0:T(8,128)(2,1)S(1)} all-gather(bf16[8,4,24,128]{3,2,1,0:T(8,128)(2,1)S(1)} %all_to_all.22), channel_id=1, replica_groups=mesh['xh'=2,'y'=4,'xl'=2,'zf'=4,'zn'=4,'c'=2] {'c'}, dimensions={0}, use_global_device_ids=true | all-gather | bytes 589824 | tf_op jit(solution)/shard_map/all_gather | solution.py:290
  49.3 0.0 copy-done
  49.3 0.6 projection.1
  49.9 10.2 %all_to_all.23.share_ref = bf16[8,32,144]{2,1,0:T(8,128)(2,1)S(1)} all-to-all(bf16[8,32,144]{2,1,0:T(8,128)(2,1)S(1)} %projection.1), channel_id=1, replica_groups={{384,128,448,192,320,64,256,0},{385,129,449,193,321,65,257,1},{386,130,..., dimensions={0} | all-to-all | bytes 147456 | tf_op jit(solution)/shard_map/all_to_all | solution.py:292
  60.1 1.5 %synthesis.1 = bf16[144,6144]{1,0:T(8,128)(2,1)} custom-call(bf16[8,32,144]{2,1,0:T(8,128)(2,1)S(1)} %all_to_all.23.share_ref, bf16[96,6144]{1,0:T(8,128)(2,1)S(1)} %get-tuple-element.10.phase_ref), custom_call_target="tpu_custom_call" | custom-call | tf_op jit(solution)/shard_map/synthesis/pallas_call | solution.py:244
  (6 shorter events, 0.1 us)
Async XLA Ops:
  10.6 24.3 %copy-start.1 = (f32[8]{0:T(128)S(1)}, f32[8]{0:T(128)}, u32[]{:S(2)}) copy-start(f32[8]{0:T(128)} %constant.22) | copy-start | bytes 100
  10.7 38.6 %copy-start = (bf16[3,16,48,256]{3,2,1,0:T(8,128)(2,1)S(1)}, bf16[3,16,48,256]{3,2,1,0:T(8,128)(2,1)}, u32[]{:S(2)}) copy-start(bf16[3,16,48,256]{3,2,1,0:T(8,128)(2,1)} %table_ref.1) | copy-start | bytes 3538948

commit v9 on v8

--- a/solution.py
+++ b/solution.py
@@ -42,7 +42,7 @@
 
 
 def level_kernel(
-    constant_hbm, pol_hbm, tor_hbm, orders_hbm, out_ref, phase_ref, weight_ref,
+    constant_hbm, pol_hbm, tor_hbm, orders_hbm, out_ref, own_ref, phase_ref, weight_ref,
     constant_ref, pol_ref, tor_ref, orders_ref, sems,
 ):
     loads = [
@@ -80,7 +80,9 @@
         for part in range(2):
             for cut in range(degree_dev // 128):
                 block = sums[part * rows : (part + 1) * rows, cut * 128 : (cut + 1) * 128]
-                out_ref[(order * 2 + part) * (degree_dev // 128) + cut] = block.astype(jnp.bfloat16)
+                at = (order * 2 + part) * (degree_dev // 128) + cut
+                out_ref[at] = block.astype(jnp.bfloat16)
+                own_ref[at] = block
 
 
 def halves(x):
@@ -106,10 +108,11 @@
     order = jnp.zeros((order_count, 128), jnp.int32)
     for at in range(order_count):
         order = jnp.where(row == at, orders_ref[at], order)
+    half_turn = (1 - 2 * (order & 1)).astype(jnp.float32).astype(jnp.bfloat16)
     order = order.astype(jnp.float32)
     first = order * lane
     quarter = points // 4
-    for start in range(0, points, 128):
+    for start in range(0, points // 2, 128):
         turn = first + order * float(start)
         quarters = jnp.floor(turn * (1.0 / quarter) + 0.5)
         x = (turn - quarters * float(quarter)) * (2.0 * math.pi / points)
@@ -125,7 +128,10 @@
         cos_high, cos_low = halves(cos_row)
         sin_high, sin_low = halves(sin_row)
         for at, rows in enumerate([cos_high, sin_high, cos_low, sin_low, cos_high, sin_high]):
-            phase_ref[at * order_count : (at + 1) * order_count, start : start + 128] = rows
+            place = slice(at * order_count, (at + 1) * order_count)
+            phase_ref[place, start : start + 128] = rows
+            start_2 = start + points // 2
+            phase_ref[place, start_2 : start_2 + 128] = rows * half_turn
 
 
 def near_place():
@@ -143,11 +149,12 @@
         level_kernel,
         out_shape=(
             pltpu.VMEM((order_count * 2 * degree_dev // 128, 3 * SHELLS, 128), jnp.bfloat16),
+            pltpu.VMEM((order_count * 2 * degree_dev // 128, 3 * SHELLS, 128), jnp.float32),
             pltpu.VMEM((6 * order_count, NPHI), jnp.bfloat16),
             pltpu.VMEM((degree_dev // 128, 128), jnp.float32),
         ),
         in_specs=[pl.BlockSpec(memory_space=pltpu.HBM)] * 4,
-        out_specs=[pl.BlockSpec(memory_space=pltpu.VMEM)] * 3,
+        out_specs=[pl.BlockSpec(memory_space=pltpu.VMEM)] * 4,
         scratch_shapes=[
             pltpu.VMEM(constants.shape, jnp.float32),
             pltpu.VMEM(poloidal.shape, jnp.bfloat16),
@@ -261,11 +268,14 @@
     blocks = half * 2 * degree_dev // 128
     near_count = lax.axis_size(NEAR)
     far_count = lax.axis_size("zf")
-    first_block = lax.axis_index("c") * blocks
-    partial, phases, weight = level_sums(poloidal, toroidal, orders)
+    core = lax.axis_index("c")
+    partial, own, phases, weight = level_sums(poloidal, toroidal, orders)
     pair = lax.all_gather(partial, "c", axis=0)
-    pair = lax.dynamic_slice_in_dim(pair, first_block, blocks, 1).astype(jnp.float32)
-    partial = (pair[0] + pair[1]).astype(jnp.bfloat16)
+    partner = lax.dynamic_slice(
+        pair, (1 - core, core * blocks, 0, 0), (1, blocks) + pair.shape[2:]
+    )
+    own = lax.dynamic_slice_in_dim(own, core * blocks, blocks, 0)
+    partial = (own + partner[0].astype(jnp.float32)).astype(jnp.bfloat16)
     shares = lax.all_to_all(partial, NEAR, 0, 0, axis_index_groups=[NEAR_ORDER], tiled=True)
     shares = shares.reshape(near_count, -1, 3 * SHELLS, 128).astype(jnp.float32)
     near_sum = lax.optimization_barrier(jnp.sum(shares, axis=0))

time: 61.9 us -> 61.6 us (level)
  no operation moved by 1% of the time
where the time goes in v9:
time: 61.6 us; the launch traced here: 61.3 us
  blocking collectives  57.4 us (93%)
  Pallas kernels  3.6 us (6%)
    all_to_all x1, blocking collectives, on_device(): lax.all_to_all(copies, 'zf', 0, 0, axis_index_groups=[FAR_ORDER], tiled=T...  15 us
    all_to_all x1, blocking collectives, on_device(): lax.all_to_all(fourier, TAB, 0, 0, axis_index_groups=[TAB_ORDER], tiled=T...  10.2 us
    all_to_all x1, blocking collectives, on_device(): lax.all_to_all(partial, NEAR, 0, 0, axis_index_groups=[NEAR_ORDER], tiled...  9.13 us
    all_gather x1, blocking collectives, on_device(): pair = lax.all_gather(partial, 'c', axis=0)  8.87 us
    all_to_all x1, blocking collectives, on_device(): lax.all_to_all(spectra, NEAR, 0, 0, axis_index_groups=[NEAR_ORDER], tiled...  8.25 us
    all_gather x1, blocking collectives, on_device(): spectra = lax.all_gather(spectra, 'c', axis=0, tiled=True)  5.92 us
    pallas_call x1, Pallas kernels, synthesis(): pl.pallas_call(synthesis_kernel, out_shape=jax.ShapeDtypeStruct((rows, po...  1.54 us
    pallas_call x1, Pallas kernels, level_sums(): pl.pallas_call(level_kernel, out_shape=(pltpu.VMEM((order_count * 2 * deg...  1.47 us

profile of v9, /device:TPU:1, one launch (start us, length us, event | category | flops | bytes accessed | tf_op | source)
XLA Modules:
  0.0 61.3 jit_solution(7899927273725021920)
XLA Ops:
  0.0 1.5 %level_sums.1 = (bf16[64,24,128]{2,1,0:T(8,128)(2,1)S(1)}, f32[64,24,128]{2,1,0:T(8,128)S(1)}, bf16[96,6144]{1,0:T(8,128)(2,1)S(1)}, f32[2,128]{1,0:T(2,128)S(1)}) custom-call(f32[2,2,48,128]{3,2,1,0:T(8,128)} %constant.21.clone.constant_hbm, bf16[16,16,2,256]{3,2,1,0:T(2,128)(2,1)} %pol_hbm.1, bf16[16,16,2,256]{3,2,1,0:T(2,128)(2,1)} %tor_hbm.1, s32[16]{0:T(128)} %orders_hbm.1), custom_call_target="tpu_custom_call" | custom-call | tf_op jit(solution)/shard_map/level_sums/pallas_call | solution.py:148
  1.5 8.9 %all-gather = bf16[128,24,128]{2,1,0:T(8,128)(2,1)S(1)} all-gather(bf16[64,24,128]{2,1,0:T(8,128)(2,1)S(1)} %get-tuple-element.11), channel_id=2, replica_groups=mesh['xh'=2,'y'=4,'xl'=2,'zf'=4,'zn'=4,'c'=2] {'c'}, dimensions={0}, use_global_device_ids=true | all-gather | bytes 1179648 | tf_op jit(solution)/shard_map/all_gather | solution.py:273
  10.4 0.0 copy-start.1
  10.4 0.0 copy-start
  10.4 9.1 %all_to_all.20 = bf16[32,24,128]{2,1,0:T(8,128)(2,1)S(1)} all-to-all(bf16[32,24,128]{2,1,0:T(8,128)(2,1)S(1)} %fusion), channel_id=1, replica_groups={{34,36,38,32,2,4,6,0},{35,37,39,33,3,5,7,1},{42,44,46,40,10,12,14,8},{4..., dimensions={0} | all-to-all | bytes 393216 | tf_op jit(solution)/shard_map/all_to_all | solution.py:279
  19.6 15.0 %all_to_all.21 = bf16[4,4,24,128]{3,2,1,0:T(8,128)(2,1)S(1)} all-to-all(bf16[4,4,24,128]{3,2,1,0:T(8,128)(2,1)S(1)} %broadcast_in_dim.4), channel_id=1, replica_groups={{16,24,0,8},{17,25,1,9},{18,26,2,10},{19,27,3,11},{20,28,4,12},{21,29,5..., dimensions={0} | all-to-all | bytes 196608 | tf_op jit(solution)/shard_map/all_to_all | solution.py:283
  34.7 0.0 copy-done.1
  34.7 0.1 multiply_convert_fusion
  34.8 8.3 %all_to_all.22 = bf16[8,4,24,128]{3,2,1,0:T(8,128)(2,1)S(1)} all-to-all(bf16[8,4,24,128]{3,2,1,0:T(8,128)(2,1)S(1)} %broadcast_in_dim.10), channel_id=1, replica_groups={{34,36,38,32,2,4,6,0},{35,37,39,33,3,5,7,1},{42,44,46,40,10,12,14,8},{4..., dimensions={0} | all-to-all | bytes 393216 | tf_op jit(solution)/shard_map/all_to_all | solution.py:299
  43.0 5.9 %all_gather.11.spectra_ref = bf16[16,4,24,128]{3,2,1,0:T(8,128)(2,1)S(1)} all-gather(bf16[8,4,24,128]{3,2,1,0:T(8,128)(2,1)S(1)} %all_to_all.22), channel_id=1, replica_groups=mesh['xh'=2,'y'=4,'xl'=2,'zf'=4,'zn'=4,'c'=2] {'c'}, dimensions={0}, use_global_device_ids=true | all-gather | bytes 589824 | tf_op jit(solution)/shard_map/all_gather | solution.py:300
  49.0 0.0 copy-done
  49.0 0.6 projection.1
  49.6 10.2 %all_to_all.23.share_ref = bf16[8,32,144]{2,1,0:T(8,128)(2,1)S(1)} all-to-all(bf16[8,32,144]{2,1,0:T(8,128)(2,1)S(1)} %projection.1), channel_id=1, replica_groups={{384,128,448,192,320,64,256,0},{385,129,449,193,321,65,257,1},{386,130,..., dimensions={0} | all-to-all | bytes 147456 | tf_op jit(solution)/shard_map/all_to_all | solution.py:302
  59.8 1.5 %synthesis.1 = bf16[144,6144]{1,0:T(8,128)(2,1)} custom-call(bf16[8,32,144]{2,1,0:T(8,128)(2,1)S(1)} %all_to_all.23.share_ref, bf16[96,6144]{1,0:T(8,128)(2,1)S(1)} %get-tuple-element.12.phase_ref), custom_call_target="tpu_custom_call" | custom-call | tf_op jit(solution)/shard_map/synthesis/pallas_call | solution.py:251
  (6 shorter events, 0.1 us)
Async XLA Ops:
  10.4 24.3 %copy-start.1 = (f32[8]{0:T(128)S(1)}, f32[8]{0:T(128)}, u32[]{:S(2)}) copy-start(f32[8]{0:T(128)} %constant.27) | copy-start | bytes 100
  10.4 38.6 %copy-start = (bf16[3,16,48,256]{3,2,1,0:T(8,128)(2,1)S(1)}, bf16[3,16,48,256]{3,2,1,0:T(8,128)(2,1)}, u32[]{:S(2)}) copy-start(bf16[3,16,48,256]{3,2,1,0:T(8,128)(2,1)} %table_ref.1) | copy-start | bytes 3538948

commit v10 on v9

--- a/solution.py
+++ b/solution.py
@@ -56,8 +56,8 @@
             ]
         )
     ]
-    for load in loads:
-        load.start()
+    for at, load in enumerate(loads):
+        load.start(priority=at % 2)
     loads[0].wait()
     weight_rows(orders_ref, weight_ref)
     longitude_rows(orders_ref, phase_ref)
@@ -241,7 +241,7 @@
         copies.append(
             pltpu.make_async_copy(chunk_ref.at[at], out_hbm.at[:, columns], sems.at[at])
         )
-        copies[-1].start()
+        copies[-1].start(priority=at % 2)
     for copy in copies:
         copy.wait()
 

time: 61.6 us -> 61.6 us (level)
  no operation moved by 1% of the time
where the time goes in v10:
time: 61.6 us; the launch traced here: 61.3 us
  blocking collectives  57.4 us (93%)
  Pallas kernels  3.6 us (6%)
    all_to_all x1, blocking collectives, on_device(): lax.all_to_all(copies, 'zf', 0, 0, axis_index_groups=[FAR_ORDER], tiled=T...  15 us
    all_to_all x1, blocking collectives, on_device(): lax.all_to_all(fourier, TAB, 0, 0, axis_index_groups=[TAB_ORDER], tiled=T...  10.2 us
    all_to_all x1, blocking collectives, on_device(): lax.all_to_all(partial, NEAR, 0, 0, axis_index_groups=[NEAR_ORDER], tiled...  9.13 us
    all_gather x1, blocking collectives, on_device(): pair = lax.all_gather(partial, 'c', axis=0)  8.87 us
    all_to_all x1, blocking collectives, on_device(): lax.all_to_all(spectra, NEAR, 0, 0, axis_index_groups=[NEAR_ORDER], tiled...  8.25 us
    all_gather x1, blocking collectives, on_device(): spectra = lax.all_gather(spectra, 'c', axis=0, tiled=True)  5.92 us
    pallas_call x1, Pallas kernels, synthesis(): pl.pallas_call(synthesis_kernel, out_shape=jax.ShapeDtypeStruct((rows, po...  1.54 us
    pallas_call x1, Pallas kernels, level_sums(): pl.pallas_call(level_kernel, out_shape=(pltpu.VMEM((order_count * 2 * deg...  1.47 us

profile of v10, /device:TPU:1, one launch (start us, length us, event | category | flops | bytes accessed | tf_op | source)
XLA Modules:
  0.0 61.3 jit_solution(7722925475535172614)
XLA Ops:
  0.0 1.5 %level_sums.1 = (bf16[64,24,128]{2,1,0:T(8,128)(2,1)S(1)}, f32[64,24,128]{2,1,0:T(8,128)S(1)}, bf16[96,6144]{1,0:T(8,128)(2,1)S(1)}, f32[2,128]{1,0:T(2,128)S(1)}) custom-call(f32[2,2,48,128]{3,2,1,0:T(8,128)} %constant.21.clone.constant_hbm, bf16[16,16,2,256]{3,2,1,0:T(2,128)(2,1)} %pol_hbm.1, bf16[16,16,2,256]{3,2,1,0:T(2,128)(2,1)} %tor_hbm.1, s32[16]{0:T(128)} %orders_hbm.1), custom_call_target="tpu_custom_call" | custom-call | tf_op jit(solution)/shard_map/level_sums/pallas_call | solution.py:148
  1.5 8.9 %all-gather = bf16[128,24,128]{2,1,0:T(8,128)(2,1)S(1)} all-gather(bf16[64,24,128]{2,1,0:T(8,128)(2,1)S(1)} %get-tuple-element.11), channel_id=2, replica_groups=mesh['xh'=2,'y'=4,'xl'=2,'zf'=4,'zn'=4,'c'=2] {'c'}, dimensions={0}, use_global_device_ids=true | all-gather | bytes 1179648 | tf_op jit(solution)/shard_map/all_gather | solution.py:273
  10.4 0.0 copy-start.1
  10.4 0.0 copy-start
  10.4 9.1 %all_to_all.20 = bf16[32,24,128]{2,1,0:T(8,128)(2,1)S(1)} all-to-all(bf16[32,24,128]{2,1,0:T(8,128)(2,1)S(1)} %fusion), channel_id=1, replica_groups={{34,36,38,32,2,4,6,0},{35,37,39,33,3,5,7,1},{42,44,46,40,10,12,14,8},{4..., dimensions={0} | all-to-all | bytes 393216 | tf_op jit(solution)/shard_map/all_to_all | solution.py:279
  19.6 15.0 %all_to_all.21 = bf16[4,4,24,128]{3,2,1,0:T(8,128)(2,1)S(1)} all-to-all(bf16[4,4,24,128]{3,2,1,0:T(8,128)(2,1)S(1)} %broadcast_in_dim.4), channel_id=1, replica_groups={{16,24,0,8},{17,25,1,9},{18,26,2,10},{19,27,3,11},{20,28,4,12},{21,29,5..., dimensions={0} | all-to-all | bytes 196608 | tf_op jit(solution)/shard_map/all_to_all | solution.py:283
  34.7 0.0 copy-done.1
  34.7 0.1 multiply_convert_fusion
  34.8 8.3 %all_to_all.22 = bf16[8,4,24,128]{3,2,1,0:T(8,128)(2,1)S(1)} all-to-all(bf16[8,4,24,128]{3,2,1,0:T(8,128)(2,1)S(1)} %broadcast_in_dim.10), channel_id=1, replica_groups={{34,36,38,32,2,4,6,0},{35,37,39,33,3,5,7,1},{42,44,46,40,10,12,14,8},{4..., dimensions={0} | all-to-all | bytes 393216 | tf_op jit(solution)/shard_map/all_to_all | solution.py:299
  43.0 5.9 %all_gather.11.spectra_ref = bf16[16,4,24,128]{3,2,1,0:T(8,128)(2,1)S(1)} all-gather(bf16[8,4,24,128]{3,2,1,0:T(8,128)(2,1)S(1)} %all_to_all.22), channel_id=1, replica_groups=mesh['xh'=2,'y'=4,'xl'=2,'zf'=4,'zn'=4,'c'=2] {'c'}, dimensions={0}, use_global_device_ids=true | all-gather | bytes 589824 | tf_op jit(solution)/shard_map/all_gather | solution.py:300
  49.0 0.0 copy-done
  49.0 0.6 projection.1
  49.6 10.2 %all_to_all.23.share_ref = bf16[8,32,144]{2,1,0:T(8,128)(2,1)S(1)} all-to-all(bf16[8,32,144]{2,1,0:T(8,128)(2,1)S(1)} %projection.1), channel_id=1, replica_groups={{384,128,448,192,320,64,256,0},{385,129,449,193,321,65,257,1},{386,130,..., dimensions={0} | all-to-all | bytes 147456 | tf_op jit(solution)/shard_map/all_to_all | solution.py:302
  59.8 1.5 %synthesis.1 = bf16[144,6144]{1,0:T(8,128)(2,1)} custom-call(bf16[8,32,144]{2,1,0:T(8,128)(2,1)S(1)} %all_to_all.23.share_ref, bf16[96,6144]{1,0:T(8,128)(2,1)S(1)} %get-tuple-element.12.phase_ref), custom_call_target="tpu_custom_call" | custom-call | tf_op jit(solution)/shard_map/synthesis/pallas_call | solution.py:251
  (6 shorter events, 0.1 us)
Async XLA Ops:
  10.4 24.3 %copy-start.1 = (f32[8]{0:T(128)S(1)}, f32[8]{0:T(128)}, u32[]{:S(2)}) copy-start(f32[8]{0:T(128)} %constant.27) | copy-start | bytes 100
  10.4 38.6 %copy-start = (bf16[3,16,48,256]{3,2,1,0:T(8,128)(2,1)S(1)}, bf16[3,16,48,256]{3,2,1,0:T(8,128)(2,1)}, u32[]{:S(2)}) copy-start(bf16[3,16,48,256]{3,2,1,0:T(8,128)(2,1)} %table_ref.1) | copy-start | bytes 3538948
